TPU v7x, 128 devices: a whole 4x4x4 slice. The times are simulated.
128 devices in a mesh: dp: 8 (over z, core), fsdp: 16 (over y, x).
Axes of the slice: x: 4, y: 4, z: 4, core: 2. Of those that a mesh axis runs over, the one named last changes fastest.
Arguments:
- patches: bfloat16 [65536, 768], P(('dp', 'fsdp')), may hold values from -6 to 6
- lengths: int32 [256, 4], P(('dp', 'fsdp')), may hold values from 1 to 128, 256 in all within a row
- skipped: int32 [65536, 1], P(('dp', 'fsdp')), may hold values 0 or 1
- strip_order: int32 [8, 16], P('dp'), may hold values from 0 to 15, each once within a row
- decoder_grad: bfloat16 [541696, 512], P(('dp', 'fsdp')), may hold values from -6 to 6
- qkv_weight: bfloat16 [768, 2304], P(('dp', 'fsdp')), may hold values from -0.21875 to 0.21875
- out_weight: bfloat16 [768, 768], P(('dp', 'fsdp')), may hold values from -0.625 to 0.625
- up_weight: bfloat16 [768, 3072], P(('dp', 'fsdp')), may hold values from -0.21875 to 0.21875
- down_weight: bfloat16 [3072, 768], P(('dp', 'fsdp')), may hold values from -0.109375 to 0.109375
- embed_weight: bfloat16 [768, 512], P(('dp', 'fsdp')), may hold values from -0.21875 to 0.21875
- gain_one: bfloat16 [768], P(('dp', 'fsdp')), may hold values from 0.5 to 1.5
- shift_one: bfloat16 [768], P(('dp', 'fsdp')), may hold values from -1.5 to 1.5
- gain_two: bfloat16 [768], P(('dp', 'fsdp')), may hold values from 0.5 to 1.5
- shift_two: bfloat16 [768], P(('dp', 'fsdp')), may hold values from -1.5 to 1.5
- bias_query: bfloat16 [768], P(('dp', 'fsdp')), may hold values from -1.5 to 1.5
- bias_value: bfloat16 [768], P(('dp', 'fsdp')), may hold values from -1.5 to 1.5
- bias_out: bfloat16 [768], P(('dp', 'fsdp')), may hold values from -1.5 to 1.5
- bias_up: bfloat16 [3072], P(('dp', 'fsdp')), may hold values from -1.5 to 1.5
- bias_down: bfloat16 [768], P(('dp', 'fsdp')), may hold values from -1.5 to 1.5
- bias_embed: bfloat16 [512], P(('dp', 'fsdp')), may hold values from -1.5 to 1.5
- mask_token: bfloat16 [512], P(('dp', 'fsdp')), may hold values from -4 to 4
Outputs:
- decoder_in: bfloat16 [541696, 512], P(('dp', 'fsdp'))
- patch_grad: float32 [65536, 768], P(('dp', 'fsdp'))
- grad_qkv: float32 [768, 2304], P(('dp', 'fsdp'))
- grad_out: float32 [768, 768], P(('dp', 'fsdp'))
- grad_up: float32 [768, 3072], P(('dp', 'fsdp'))
- grad_down: float32 [3072, 768], P(('dp', 'fsdp'))
- grad_embed: float32 [768, 512], P(('dp', 'fsdp'))
- grad_gain_one: float32 [768], P(('dp', 'fsdp'))
- grad_shift_one: float32 [768], P(('dp', 'fsdp'))
- grad_gain_two: float32 [768], P(('dp', 'fsdp'))
- grad_shift_two: float32 [768], P(('dp', 'fsdp'))
- grad_bias_query: float32 [768], P(('dp', 'fsdp'))
- grad_bias_value: float32 [768], P(('dp', 'fsdp'))
- grad_bias_out: float32 [768], P(('dp', 'fsdp'))
- grad_bias_up: float32 [3072], P(('dp', 'fsdp'))
- grad_bias_down: float32 [768], P(('dp', 'fsdp'))
- grad_bias_embed: float32 [512], P(('dp', 'fsdp'))
- grad_mask_token: float32 [512], P(('dp', 'fsdp'))
Inputs may be any that keep to these rules, and one draw needn't show every extreme that they name: `lengths`: each row sums to 256; the longest strip of every row has exactly 128 rows. `strip_order`: each row is a permutation of 0 to 15.
All inputs are finite; a program needn't handle non-finite values. No bound on the sum of `skipped` on one device may be relied on, other than what follows from the above.
Results may differ from a plain program's by a relative error of at most 0.015.
Values may be sent and summed in bfloat16 or wider, within the bound.
A program may use at most 192 MiB of HBM per device.

v0:
```python
import jax
import jax.numpy as jnp
from jax import lax
from jax.sharding import PartitionSpec as P

HEADS = 12
STRIP_POS = 529


epsilon = 1e-06
masked_score = -1000000000.0
code_base = 32


def matmul(left, right):
    return jnp.dot(left, right, preferred_element_type=jnp.float32)


def left_t(left, right):
    return lax.dot_general(
        left, right, (((0,), (0,)), ((), ())), preferred_element_type=jnp.float32
    )


def right_t(left, right):
    return lax.dot_general(
        left, right, (((1,), (1,)), ((), ())), preferred_element_type=jnp.float32
    )


def norm_rows(values, gain, shift):
    center = values - jnp.mean(values, -1, keepdims=True)
    factor = lax.rsqrt(jnp.mean(center * center, -1, keepdims=True) + epsilon)
    normed = center * factor
    return (normed * gain + shift, normed, factor)


def norm_back(grad_norm, gain, normed, factor):
    scaled = grad_norm * gain
    first = jnp.mean(scaled, -1, keepdims=True)
    second = jnp.mean(scaled * normed, -1, keepdims=True)
    return factor * (scaled - first - normed * second)


def gelu_slope(values):
    cumulative = 0.5 * (1.0 + lax.erf(values * 0.7071067811865476))
    density = jnp.exp(-0.5 * values * values) * 0.3989422804014327
    return cumulative + values * density


def doc_ids(row_lengths, count):
    bounds = jnp.cumsum(row_lengths)
    places = lax.broadcasted_iota(jnp.int32, (count, bounds.shape[0]), 0)
    return jnp.sum((places >= bounds[None, :]).astype(jnp.int32), -1)


def strip_places(row_lengths, skip_block, count):
    doc_block = doc_ids(row_lengths, count)
    starts = jnp.cumsum(row_lengths) - row_lengths
    doc_hot = (
        doc_block[:, None] == lax.broadcasted_iota(jnp.int32, (1, row_lengths.shape[0]), 1)
    ).astype(jnp.int32)
    start_row = jnp.sum(doc_hot * starts[None, :], -1)
    through = jnp.cumsum(skip_block)
    before = through - skip_block
    base_row = jnp.sum(doc_hot * jnp.take(before, starts)[None, :], -1)
    within = lax.broadcasted_iota(jnp.int32, (count,), 0) - start_row
    return (doc_block, within, within + through - base_row)


def split_heads(packed, heads):
    count = packed.shape[0]
    width = packed.shape[1] // 3
    return [
        packed[:, third * width : (third + 1) * width].reshape(count, heads, width // heads)
        for third in range(3)
    ]


def attend_forward(packed, same_doc, heads):
    queries, keys_in, values_in = split_heads(packed, heads)
    factor = queries.shape[2] ** (-0.5)
    scores = (
        jnp.einsum("qhd,khd->hqk", queries, keys_in, preferred_element_type=jnp.float32) * factor
    )
    scores = jnp.where(same_doc[None], scores, masked_score)
    largest = jnp.max(scores, -1, keepdims=True)
    shifted = jnp.exp(scores - largest)
    sums_exp = jnp.sum(shifted, -1, keepdims=True)
    weights = (shifted / sums_exp).astype(jnp.bfloat16)
    context = jnp.einsum("hqk,khd->qhd", weights, values_in, preferred_element_type=jnp.float32)
    return (context.reshape(packed.shape[0], -1), largest + jnp.log(sums_exp))


def attend_back(packed, same_doc, log_sums, context_grad, heads):
    queries, keys_in, values_in = split_heads(packed, heads)
    count, head_count, head_size = queries.shape
    factor = head_size ** (-0.5)
    scores = (
        jnp.einsum("qhd,khd->hqk", queries, keys_in, preferred_element_type=jnp.float32) * factor
    )
    scores = jnp.where(same_doc[None], scores, masked_score)
    weights = jnp.exp(scores - log_sums)
    weights_low = weights.astype(jnp.bfloat16)
    grad_ctx = context_grad.reshape(count, head_count, head_size)
    grad_weights = jnp.einsum(
        "qhd,khd->hqk", grad_ctx, values_in, preferred_element_type=jnp.float32
    )
    inner = jnp.sum(weights * grad_weights, -1, keepdims=True)
    grad_scores = (weights * (grad_weights - inner)).astype(jnp.bfloat16)
    grad_query = (
        jnp.einsum("hqk,khd->qhd", grad_scores, keys_in, preferred_element_type=jnp.float32)
        * factor
    )
    grad_key = (
        jnp.einsum("hqk,qhd->khd", grad_scores, queries, preferred_element_type=jnp.float32)
        * factor
    )
    grad_value = jnp.einsum(
        "hqk,qhd->khd", weights_low, grad_ctx, preferred_element_type=jnp.float32
    )
    return jnp.concatenate(
        [grad_query.reshape(count, -1), grad_key.reshape(count, -1), grad_value.reshape(count, -1)],
        -1,
    )


def forward_block(params, rows, same_doc, heads):
    (
        full_qkv,
        full_out,
        full_up,
        full_down,
        full_embed,
        gain_first,
        shift_first,
        gain_second,
        shift_second,
        query_bias,
        value_bias,
        out_bias,
        up_bias,
        down_bias,
        embed_bias,
        mask_full,
    ) = params
    normed_one, hat_one, factor_one = norm_rows(
        rows, gain_first.astype(jnp.float32), shift_first.astype(jnp.float32)
    )
    low_one = normed_one.astype(jnp.bfloat16)
    bias_qkv = jnp.concatenate([query_bias, jnp.zeros_like(query_bias), value_bias]).astype(
        jnp.float32
    )
    packed = (matmul(low_one, full_qkv) + bias_qkv).astype(jnp.bfloat16)
    context, log_sums = attend_forward(packed, same_doc, heads)
    context_low = context.astype(jnp.bfloat16)
    middle = rows + matmul(context_low, full_out) + out_bias.astype(jnp.float32)
    normed_two, hat_two, factor_two = norm_rows(
        middle, gain_second.astype(jnp.float32), shift_second.astype(jnp.float32)
    )
    low_two = normed_two.astype(jnp.bfloat16)
    hidden = matmul(low_two, full_up) + up_bias.astype(jnp.float32)
    active_low = jax.nn.gelu(hidden, approximate=False).astype(jnp.bfloat16)
    final_rows = middle + matmul(active_low, full_down) + down_bias.astype(jnp.float32)
    final_low = final_rows.astype(jnp.bfloat16)
    embedded = (matmul(final_low, full_embed) + embed_bias.astype(jnp.float32)).astype(jnp.bfloat16)
    stored = (
        same_doc,
        hat_one,
        factor_one,
        low_one,
        packed,
        log_sums,
        context_low,
        hat_two,
        factor_two,
        low_two,
        hidden,
        active_low,
        final_low,
    )
    return (embedded, stored)


def backward_block(params, stored, grad_embedded, heads):
    (
        full_qkv,
        full_out,
        full_up,
        full_down,
        full_embed,
        gain_first,
        shift_first,
        gain_second,
        shift_second,
        query_bias,
        value_bias,
        out_bias,
        up_bias,
        down_bias,
        embed_bias,
        mask_full,
    ) = params
    (
        same_doc,
        hat_one,
        factor_one,
        low_one,
        packed,
        log_sums,
        context_low,
        hat_two,
        factor_two,
        low_two,
        hidden,
        active_low,
        final_low,
    ) = stored
    width = hat_one.shape[1]
    embed_low = grad_embedded.astype(jnp.bfloat16)
    grad_final = right_t(embed_low, full_embed)
    down_low = grad_final.astype(jnp.bfloat16)
    grad_active = right_t(down_low, full_down)
    hidden_low = (grad_active * gelu_slope(hidden)).astype(jnp.bfloat16)
    grad_two = right_t(hidden_low, full_up)
    grad_middle = grad_final + norm_back(
        grad_two, gain_second.astype(jnp.float32), hat_two, factor_two
    )
    attn_low = grad_middle.astype(jnp.bfloat16)
    context_grad = right_t(attn_low, full_out).astype(jnp.bfloat16)
    packed_grad = attend_back(packed, same_doc, log_sums, context_grad, heads).astype(jnp.bfloat16)
    grad_one = right_t(packed_grad, full_qkv)
    grad_rows = grad_middle + norm_back(
        grad_one, gain_first.astype(jnp.float32), hat_one, factor_one
    )
    packed_wide = packed_grad.astype(jnp.float32)
    grads = (
        left_t(low_one, packed_grad),
        left_t(context_low, attn_low),
        left_t(low_two, hidden_low),
        left_t(active_low, down_low),
        left_t(final_low, embed_low),
        jnp.sum(grad_one * hat_one, 0),
        jnp.sum(grad_one, 0),
        jnp.sum(grad_two * hat_two, 0),
        jnp.sum(grad_two, 0),
        jnp.sum(packed_wide[:, :width], 0),
        jnp.sum(packed_wide[:, 2 * width :], 0),
        jnp.sum(grad_middle, 0),
        jnp.sum(hidden_low.astype(jnp.float32), 0),
        jnp.sum(grad_final, 0),
        jnp.sum(grad_embedded, 0),
    )
    return (grads, grad_rows)


def on_device(
    patches,
    lengths,
    skipped,
    strip_order,
    decoder_grad,
    qkv_weight,
    out_weight,
    up_weight,
    down_weight,
    embed_weight,
    gain_one,
    shift_one,
    gain_two,
    shift_two,
    bias_query,
    bias_value,
    bias_out,
    bias_up,
    bias_down,
    bias_embed,
    mask_token,
):
    shards = (
        qkv_weight,
        out_weight,
        up_weight,
        down_weight,
        embed_weight,
        gain_one,
        shift_one,
        gain_two,
        shift_two,
        bias_query,
        bias_value,
        bias_out,
        bias_up,
        bias_down,
        bias_embed,
        mask_token,
    )
    micro_count = lengths.shape[0]
    strip_count = lengths.shape[1]
    rows_dev = patches.shape[0]
    block_rows = rows_dev // micro_count
    capacity = block_rows // 2
    owner_count = lax.axis_size("fsdp")
    own_index = lax.axis_index("fsdp")
    strips_dev = micro_count * strip_count
    order_row = strip_order[0]
    kept_blocks = []
    embedded_blocks = []
    within_blocks = []
    position_blocks = []
    strip_blocks = []
    for block_index in range(micro_count):
        params = (
            lax.all_gather(shards[0], ("dp", "fsdp"), axis=0, tiled=True),
            lax.all_gather(shards[1], ("dp", "fsdp"), axis=0, tiled=True),
            lax.all_gather(shards[2], ("dp", "fsdp"), axis=0, tiled=True),
            lax.all_gather(shards[3], ("dp", "fsdp"), axis=0, tiled=True),
            lax.all_gather(shards[4], ("dp", "fsdp"), axis=0, tiled=True),
            lax.all_gather(shards[5], ("dp", "fsdp"), axis=0, tiled=True),
            lax.all_gather(shards[6], ("dp", "fsdp"), axis=0, tiled=True),
            lax.all_gather(shards[7], ("dp", "fsdp"), axis=0, tiled=True),
            lax.all_gather(shards[8], ("dp", "fsdp"), axis=0, tiled=True),
            lax.all_gather(shards[9], ("dp", "fsdp"), axis=0, tiled=True),
            lax.all_gather(shards[10], ("dp", "fsdp"), axis=0, tiled=True),
            lax.all_gather(shards[11], ("dp", "fsdp"), axis=0, tiled=True),
            lax.all_gather(shards[12], ("dp", "fsdp"), axis=0, tiled=True),
            lax.all_gather(shards[13], ("dp", "fsdp"), axis=0, tiled=True),
            lax.all_gather(shards[14], ("dp", "fsdp"), axis=0, tiled=True),
            lax.all_gather(shards[15], ("dp", "fsdp"), axis=0, tiled=True),
        )
        skip_block = skipped[block_index * block_rows : (block_index + 1) * block_rows, 0]
        doc_block, within, position = strip_places(lengths[block_index], skip_block, block_rows)
        within_blocks.append(within)
        position_blocks.append(position)
        strip_blocks.append(block_index * strip_count + doc_block)
        same_doc = doc_block[:, None] == doc_block[None, :]
        rows = patches[block_index * block_rows : (block_index + 1) * block_rows].astype(
            jnp.float32
        )
        embedded, stored = forward_block(params, rows, same_doc, HEADS)
        embedded_blocks.append(embedded)
        kept_blocks.append(stored)
    mask_full = params[15]
    embedded_all = jnp.concatenate(embedded_blocks, 0)
    within_all = jnp.concatenate(within_blocks, 0)
    position_all = jnp.concatenate(position_blocks, 0)
    strip_all = jnp.concatenate(strip_blocks, 0)
    strip_hot = (strip_all[:, None] == lax.broadcasted_iota(jnp.int32, (1, owner_count), 1)).astype(
        jnp.int32
    )
    owner_row = (own_index + jnp.sum(strip_hot * order_row[None, :], -1)) % owner_count
    slots = owner_row * capacity + within_all
    placing = (
        slots[None, :] == lax.broadcasted_iota(jnp.int32, (owner_count * capacity, rows_dev), 0)
    ).astype(jnp.bfloat16)
    outgoing = matmul(placing, embedded_all).astype(jnp.bfloat16).reshape(owner_count, capacity, -1)
    code_high = (position_all // code_base + 1).astype(jnp.bfloat16)[:, None]
    code_low = (position_all % code_base).astype(jnp.bfloat16)[:, None]
    high_sent = matmul(placing, code_high).astype(jnp.bfloat16).reshape(owner_count, capacity)
    low_sent = matmul(placing, code_low).astype(jnp.bfloat16).reshape(owner_count, capacity)
    arrived, high_got, low_got = (
        lax.all_to_all(outgoing, "fsdp", split_axis=0, concat_axis=0, tiled=True),
        lax.all_to_all(high_sent, "fsdp", split_axis=0, concat_axis=0, tiled=True),
        lax.all_to_all(low_sent, "fsdp", split_axis=0, concat_axis=0, tiled=True),
    )
    total_slots = decoder_grad.shape[0]
    sender = lax.broadcasted_iota(jnp.int32, (owner_count, strips_dev), 0)
    strip_ids = lax.broadcasted_iota(jnp.int32, (owner_count, strips_dev), 1)
    match = ((sender + order_row[None, :strips_dev]) % owner_count == own_index).astype(jnp.int32)
    strip_of = jnp.sum(match * strip_ids, -1)
    high_int = high_got.astype(jnp.int32)
    present = high_int > 0
    place_at = jnp.where(
        present,
        strip_of[:, None] * STRIP_POS + (high_int - 1) * code_base + low_got.astype(jnp.int32),
        total_slots,
    ).reshape(-1)
    placed = (
        jnp.zeros((total_slots, arrived.shape[2]), jnp.bfloat16)
        .at[place_at]
        .set(arrived.reshape(-1, arrived.shape[2]), mode="drop")
    )
    filled = jnp.zeros((total_slots,), jnp.float32).at[place_at].set(1.0, mode="drop")[:, None]
    decoder_in = jnp.where(filled > 0.5, placed, mask_full[None, :])
    cotangent = decoder_grad.astype(jnp.float32)
    mask_grad = jnp.sum((1.0 - filled) * cotangent, 0)
    picked = jnp.take(cotangent, jnp.minimum(place_at, total_slots - 1), axis=0)
    returning = (
        (picked * present.reshape(-1, 1).astype(jnp.float32))
        .astype(jnp.bfloat16)
        .reshape(owner_count, capacity, -1)
    )
    returned = lax.all_to_all(returning, "fsdp", split_axis=0, concat_axis=0, tiled=True)
    grad_embedded = left_t(placing, returned.reshape(owner_count * capacity, -1))
    summed = None
    row_grads = [None] * micro_count
    for block_index in reversed(range(micro_count)):
        params = (
            lax.all_gather(shards[0], ("dp", "fsdp"), axis=0, tiled=True),
            lax.all_gather(shards[1], ("dp", "fsdp"), axis=0, tiled=True),
            lax.all_gather(shards[2], ("dp", "fsdp"), axis=0, tiled=True),
            lax.all_gather(shards[3], ("dp", "fsdp"), axis=0, tiled=True),
            lax.all_gather(shards[4], ("dp", "fsdp"), axis=0, tiled=True),
            lax.all_gather(shards[5], ("dp", "fsdp"), axis=0, tiled=True),
            lax.all_gather(shards[6], ("dp", "fsdp"), axis=0, tiled=True),
            lax.all_gather(shards[7], ("dp", "fsdp"), axis=0, tiled=True),
            lax.all_gather(shards[8], ("dp", "fsdp"), axis=0, tiled=True),
            lax.all_gather(shards[9], ("dp", "fsdp"), axis=0, tiled=True),
            lax.all_gather(shards[10], ("dp", "fsdp"), axis=0, tiled=True),
            lax.all_gather(shards[11], ("dp", "fsdp"), axis=0, tiled=True),
            lax.all_gather(shards[12], ("dp", "fsdp"), axis=0, tiled=True),
            lax.all_gather(shards[13], ("dp", "fsdp"), axis=0, tiled=True),
            lax.all_gather(shards[14], ("dp", "fsdp"), axis=0, tiled=True),
            lax.all_gather(shards[15], ("dp", "fsdp"), axis=0, tiled=True),
        )
        grads, grad_rows = backward_block(
            params,
            kept_blocks[block_index],
            grad_embedded[block_index * block_rows : (block_index + 1) * block_rows],
            HEADS,
        )
        summed = grads if summed is None else jax.tree.map(jnp.add, summed, grads)
        row_grads[block_index] = grad_rows
    shares = lax.psum_scatter(
        summed + (mask_grad,), ("dp", "fsdp"), scatter_dimension=0, tiled=True
    )
    return (decoder_in, jnp.concatenate(row_grads, 0)) + tuple(shares)


def solution(mesh):
    return jax.shard_map(
        on_device,
        mesh=mesh,
        in_specs=(
            P(("dp", "fsdp"), None),
            P(("dp", "fsdp"), None),
            P(("dp", "fsdp"), None),
            P("dp", None),
            P(("dp", "fsdp"), None),
            P(("dp", "fsdp"), None),
            P(("dp", "fsdp"), None),
            P(("dp", "fsdp"), None),
            P(("dp", "fsdp"), None),
            P(("dp", "fsdp"), None),
            P(("dp", "fsdp")),
            P(("dp", "fsdp")),
            P(("dp", "fsdp")),
            P(("dp", "fsdp")),
            P(("dp", "fsdp")),
            P(("dp", "fsdp")),
            P(("dp", "fsdp")),
            P(("dp", "fsdp")),
            P(("dp", "fsdp")),
            P(("dp", "fsdp")),
            P(("dp", "fsdp")),
        ),
        out_specs=(
            P(("dp", "fsdp"), None),
            P(("dp", "fsdp"), None),
            P(("dp", "fsdp"), None),
            P(("dp", "fsdp"), None),
            P(("dp", "fsdp"), None),
            P(("dp", "fsdp"), None),
            P(("dp", "fsdp"), None),
            P(("dp", "fsdp")),
            P(("dp", "fsdp")),
            P(("dp", "fsdp")),
            P(("dp", "fsdp")),
            P(("dp", "fsdp")),
            P(("dp", "fsdp")),
            P(("dp", "fsdp")),
            P(("dp", "fsdp")),
            P(("dp", "fsdp")),
            P(("dp", "fsdp")),
            P(("dp", "fsdp")),
        ),
        check_vma=False,
    )
```

profile of v0, /device:TPU:0, one launch (start us, length us, event | category | flops | bytes accessed | tf_op | source)
XLA Modules:
  0.0 1377.6 jit_solution(4995110812872440784)
XLA Ops:
  17.9 7.1 all-to-all-start
  27.8 6.8 convert_element_type.306
  34.6 7.2 all-to-all-start.1
  41.9 7.4 all-to-all-done.1
  50.1 13.0 gather_fusion
  71.4 81.8 %all-gather.3 = bf16[128,6,512]{2,1,0:T(8,128)(2,1)S(1)} all-gather(bf16[1,6,512]{2,1,0:T(8,128)(2,1)S(1)} %bitcast.239), channel_id=1, replica_groups=mesh['dp'=8,'fsdp'=16] {'dp','fsdp'}, dimensions={0}, use_global_device_ids=true | all-gather | bytes 792576 | tf_op jit(solution)/shard_map/all_gather | solution.py:318
  155.8 65.6 %all-reduce.31 = (bf16[768]{0:T(1024)(128)(2,1)S(1)}, bf16[768]{0:T(1024)(128)(2,1)S(1)}, bf16[768]{0:T(1024)(128)(2,1)S(1)}, bf16[768]{0:T(1024)(128)(2,1)S(1)}...) all-reduce(bf16[768]{0:T(1024)(128)(2,1)S(1)} %dynamic-update-slice, ...), channel_id=1, replica_groups=mesh['dp'=8,'fsdp'=16] {'dp','fsdp'}, use_global_device_ids=true, to_apply=%add.3 | all-reduce | flops 10240 | bytes 40960
  234.4 6.6 reshape.634
  262.3 7.8 reshape.638
  270.1 11.8 fusion.14
  282.0 10.9 fusion.17
  371.0 403.5 %fusion.155 = (f32[8,2304]{1,0:T(8,128)}, f32[8,768]{1,0:T(8,128)S(1)}, f32[8,3072]{1,0:T(8,128)}, f32[8,512]{1,0:T(8,128)S(1)}) fusion(f32[768,2304]{1,0:T(8,128)} %convolution_add_fusion, f32[768,768]{1,0:T(8,128)} %convolution_add_fusion.7, f32[768,3072]{1,0:T(8,128)} %convolution_add_fusion.2, f32[768,512]{1,0:T(8,128)} %convolution_add_fusion.8), kind=kCustom, calls=%all-reduce-scatter.4 | all-reduce-scatter fusion | flops 6815745 | bytes 20660224
  785.0 11.4 collective-permute-start.107
  798.7 13.6 collective-permute-start.109
  828.2 8.2 scatter_custom_fusion
  879.7 6.2 collective-permute-start.34
  1026.7 13.3 collective-permute-done.24
  1040.0 11.4 collective-permute-start.29
  1116.7 62.8 %all-reduce.30 = (f32[768]{0:T(1024)S(1)}, f32[768]{0:T(1024)S(1)}, f32[768]{0:T(1024)S(1)}, f32[768]{0:T(1024)S(1)}, f32[768]{0:T(1024)S(1)}, /*index=5*/f32[76...) all-reduce(f32[768]{0:T(1024)S(1)} %add.493, ...), channel_id=7, replica_groups=mesh['dp'=8,'fsdp'=16] {'dp','fsdp'}, use_global_device_ids=true, to_apply=%region_45.47.clone | all-reduce | flops 10240 | bytes 81920
  1203.5 15.2 %concatenate.53 = f32[262,512]{1,0:T(8,128)S(1)} concatenate(f32[6,512]{1,0:T(8,128)S(1)} %copy-done.192, f32[8,512]{1,0:T(8,128)} %copy-done.219, f32[8,512]{1,0:T(8,128)} %copy-done.218, f32[8,512]{1,0:T(8,128)} %copy-done.217, f32[8,512]{1,0:T(8,128)S(1)} %copy-done.216, f32[8,512]{1,0:T(8,128)S(1)} %copy-done.214, f32[8,512]{1,0:T(8,128)S(1)} %copy-done.212, ...), dimensions={0} | concatenate | bytes 1073152
  1234.1 27.2 %concatenate.51 = f32[262,768]{1,0:T(8,128)S(1)} concatenate(f32[6,768]{1,0:T(8,128)} %copy-done.155, f32[8,768]{1,0:T(8,128)} %copy-done.186, f32[8,768]{1,0:T(8,128)} %copy-done.185, f32[8,768]{1,0:T(8,128)} %copy-done.184, f32[8,768]{1,0:T(8,128)} %copy-done.183, f32[8,768]{1,0:T(8,128)} %copy-done.182, f32[8,768]{1,0:T(8,128)} %copy-done.181, f32[8,768]{1,0:T(8,128)} %copy-done.180, ...), dimensions={0} | concatenate | bytes 1609728
  1275.1 33.5 %concatenate.50 = f32[262,2304]{1,0:T(8,128)S(1)} concatenate(f32[6,2304]{1,0:T(8,128)} %copy-done.113, f32[8,2304]{1,0:T(8,128)} %copy-done.134, f32[8,2304]{1,0:T(8,128)} %copy-done.132, f32[8,2304]{1,0:T(8,128)} %copy-done.131, f32[8,2304]{1,0:T(8,128)} %copy-done.130, f32[8,2304]{1,0:T(8,128)} %copy-done.129, f32[8,2304]{1,0:T(8,128)} %copy-done.128, f32[8,2304]{1,0:T(8,128)} %copy-done.127, ...), dimensions={0} | concatenate | bytes 4829184
  1320.6 31.5 %concatenate.52 = f32[262,3072]{1,0:T(8,128)S(1)} concatenate(f32[6,3072]{1,0:T(8,128)S(1)} %collective-permute-done.95, f32[8,3072]{1,0:T(8,128)} %collective-permute-done.94, f32[8,3072]{1,0:T(8,128)} %copy-done.110, f32[8,3072]{1,0:T(8,128)} %copy-done.109, f32[8,3072]{1,0:T(8,128)} %copy-done.108, f32[8,3072]{1,0:T(8,128)} %copy-done.107, f32[8,3072]{1,0:T(8,128)} %copy-done.106, ...), dimensions={0} | concatenate | bytes 6438912
  1352.8 12.7 scatter_custom_fusion.1
  (1046 shorter events, 481.2 us)
Async XLA Ops:
  7.2 224.0 %all-gather.13.cloned.1.call-start = ((), (), s32[]{:S(2)}) async-start(), calls=%async_computation.8 | async-start | bytes 1585152 | tf_op jit(solution)/shard_map/all_gather | solution.py:315
  7.9 226.5 %all-gather.11.cloned.1.call-start = ((), (), s32[]{:S(2)}) async-start(), calls=%async_computation.7 | async-start | bytes 4755456 | tf_op jit(solution)/shard_map/all_gather | solution.py:314
  8.7 253.7 %all-gather.15.cloned.1.call-start = ((), (), s32[]{:S(2)}) async-start(), calls=%async_computation.9 | async-start | bytes 6340608 | tf_op jit(solution)/shard_map/all_gather | solution.py:316
  25.0 267.9 %all-gather.9.cloned.1.call-start = ((), (), s32[]{:S(2)}) async-start(), calls=%async_computation.5 | async-start | bytes 4755456 | tf_op jit(solution)/shard_map/all_gather | solution.py:317
  66.8 158.9 %all-to-all-start.3 = ((bf16[16,128,512]{2,1,0:T(8,128)(2,1)}), bf16[16,128,512]{2,1,0:T(8,128)(2,1)}, u32[]{:S(2)}, u32[]{:S(2)}) async-start(bf16[16,128,512]{2,1,0:T(8,128)(2,1)} %multiply_convert_fusion), calls=%async_computation.3 | async-start | bytes 4194304 | tf_op jit(solution)/shard_map/all_to_all | solution.py:393
  71.4 1299.3 %reduce-scatter.10.cloned.1.call-start = ((), (), s32[]{:S(2)}) async-start(), calls=%async_computation.6 | async-start | bytes 9510912 | tf_op jit(solution)/shard_map/reduce_scatter | solution.py:424
  1010.9 341.9 %all-to-all-start.2 = ((bf16[16,128,512]{2,1,0:T(8,128)(2,1)}), bf16[16,128,512]{2,1,0:T(8,128)(2,1)}, u32[]{:S(2)}, u32[]{:S(2)}) async-start(bf16[16,128,512]{2,1,0:T(8,128)(2,1)} %bitcast.217), calls=%async_computation.2 | async-start | bytes 4194304 | tf_op jit(solution)/shard_map/all_to_all | solution.py:362
  1025.4 35.0 %collective-permute-start.28 = (f32[8,2304]{1,0:T(8,128)}, f32[8,2304]{1,0:T(8,128)S(1)}, u32[]{:S(2)}, u32[]{:S(2)}) collective-permute-start(f32[8,2304]{1,0:T(8,128)} %get-tuple-element.77), channel_id=1, source_target_pairs={{0,29},{1,30},{2,31},{3,32},{4,33},{5,34},{6,35},{7,36},{8,37},{9,... | collective-permute-start | bytes 221192
  1061.8 35.6 %collective-permute-start.64 = (f32[8,3072]{1,0:T(8,128)}, f32[8,3072]{1,0:T(8,128)S(1)}, u32[]{:S(2)}, u32[]{:S(2)}) collective-permute-start(f32[8,3072]{1,0:T(8,128)} %get-tuple-element.79), channel_id=1, source_target_pairs={{0,1},{1,2},{2,3},{3,4},{4,5},{5,6},{6,7},{7,8},{8,9},{9,10},{10,1... | collective-permute-start | bytes 294920
  1101.5 84.4 %collective-permute-start.70 = (f32[8,3072]{1,0:T(8,128)}, f32[8,3072]{1,0:T(8,128)S(1)}, u32[]{:S(2)}, u32[]{:S(2)}) collective-permute-start(f32[8,3072]{1,0:T(8,128)} %get-tuple-element.79), channel_id=1, source_target_pairs={{0,7},{1,8},{2,9},{3,10},{4,11},{5,12},{6,13},{7,14},{8,15},{9,16}... | collective-permute-start | bytes 294920
  1104.5 85.6 %collective-permute-start.71 = (f32[8,3072]{1,0:T(8,128)}, f32[8,3072]{1,0:T(8,128)S(1)}, u32[]{:S(2)}, u32[]{:S(2)}) collective-permute-start(f32[8,3072]{1,0:T(8,128)} %get-tuple-element.79), channel_id=1, source_target_pairs={{0,8},{1,9},{2,10},{3,11},{4,12},{5,13},{6,14},{7,15},{8,16},{9,17... | collective-permute-start | bytes 294920
  1106.8 85.1 %collective-permute-start.72 = (f32[8,3072]{1,0:T(8,128)}, f32[8,3072]{1,0:T(8,128)S(1)}, u32[]{:S(2)}, u32[]{:S(2)}) collective-permute-start(f32[8,3072]{1,0:T(8,128)} %get-tuple-element.79), channel_id=1, source_target_pairs={{0,9},{1,10},{2,11},{3,12},{4,13},{5,14},{6,15},{7,16},{8,17},{9,1... | collective-permute-start | bytes 294920
  1109.7 87.2 %collective-permute-start.73 = (f32[8,3072]{1,0:T(8,128)}, f32[8,3072]{1,0:T(8,128)S(1)}, u32[]{:S(2)}, u32[]{:S(2)}) collective-permute-start(f32[8,3072]{1,0:T(8,128)} %get-tuple-element.79), channel_id=1, source_target_pairs={{0,10},{1,11},{2,12},{3,13},{4,14},{5,15},{6,16},{7,17},{8,18},{9,... | collective-permute-start | bytes 294920
  1113.8 85.0 %collective-permute-start.74 = (f32[8,3072]{1,0:T(8,128)}, f32[8,3072]{1,0:T(8,128)S(1)}, u32[]{:S(2)}, u32[]{:S(2)}) collective-permute-start(f32[8,3072]{1,0:T(8,128)} %get-tuple-element.79), channel_id=1, source_target_pairs={{0,11},{1,12},{2,13},{3,14},{4,15},{5,16},{6,17},{7,18},{8,19},{9,... | collective-permute-start | bytes 294920
  1218.8 42.5 %collective-permute-start.80 = (f32[8,3072]{1,0:T(8,128)}, f32[8,3072]{1,0:T(8,128)S(1)}, u32[]{:S(2)}, u32[]{:S(2)}) collective-permute-start(f32[8,3072]{1,0:T(8,128)} %get-tuple-element.79), channel_id=1, source_target_pairs={{0,17},{1,18},{2,19},{3,20},{4,21},{5,22},{6,23},{7,24},{8,25},{9,... | collective-permute-start | bytes 294920
  1221.2 43.6 %collective-permute-start.81 = (f32[8,3072]{1,0:T(8,128)}, f32[8,3072]{1,0:T(8,128)S(1)}, u32[]{:S(2)}, u32[]{:S(2)}) collective-permute-start(f32[8,3072]{1,0:T(8,128)} %get-tuple-element.79), channel_id=1, source_target_pairs={{0,18},{1,19},{2,20},{3,21},{4,22},{5,23},{6,24},{7,25},{8,26},{9,... | collective-permute-start | bytes 294920
  1224.6 43.6 %collective-permute-start.82 = (f32[8,3072]{1,0:T(8,128)}, f32[8,3072]{1,0:T(8,128)S(1)}, u32[]{:S(2)}, u32[]{:S(2)}) collective-permute-start(f32[8,3072]{1,0:T(8,128)} %get-tuple-element.79), channel_id=1, source_target_pairs={{0,19},{1,20},{2,21},{3,22},{4,23},{5,24},{6,25},{7,26},{8,27},{9,... | collective-permute-start | bytes 294920
  1229.9 40.0 %collective-permute-start.83 = (f32[8,3072]{1,0:T(8,128)}, f32[8,3072]{1,0:T(8,128)S(1)}, u32[]{:S(2)}, u32[]{:S(2)}) collective-permute-start(f32[8,3072]{1,0:T(8,128)} %get-tuple-element.79), channel_id=1, source_target_pairs={{0,20},{1,21},{2,22},{3,23},{4,24},{5,25},{6,26},{7,27},{8,28},{9,... | collective-permute-start | bytes 294920
  1231.6 40.1 %collective-permute-start.84 = (f32[8,3072]{1,0:T(8,128)}, f32[8,3072]{1,0:T(8,128)S(1)}, u32[]{:S(2)}, u32[]{:S(2)}) collective-permute-start(f32[8,3072]{1,0:T(8,128)} %get-tuple-element.79), channel_id=1, source_target_pairs={{0,21},{1,22},{2,23},{3,24},{4,25},{5,26},{6,27},{7,28},{8,29},{9,... | collective-permute-start | bytes 294920
  1261.3 47.3 %collective-permute-start.85 = (f32[8,3072]{1,0:T(8,128)}, f32[8,3072]{1,0:T(8,128)S(1)}, u32[]{:S(2)}, u32[]{:S(2)}) collective-permute-start(f32[8,3072]{1,0:T(8,128)} %get-tuple-element.79), channel_id=1, source_target_pairs={{0,22},{1,23},{2,24},{3,25},{4,26},{5,27},{6,28},{7,29},{8,30},{9,... | collective-permute-start | bytes 294920
  1264.9 45.7 %collective-permute-start.86 = (f32[8,3072]{1,0:T(8,128)}, f32[8,3072]{1,0:T(8,128)S(1)}, u32[]{:S(2)}, u32[]{:S(2)}) collective-permute-start(f32[8,3072]{1,0:T(8,128)} %get-tuple-element.79), channel_id=1, source_target_pairs={{0,23},{1,24},{2,25},{3,26},{4,27},{5,28},{6,29},{7,30},{8,31},{9,... | collective-permute-start | bytes 294920
  1268.2 43.7 %collective-permute-start.87 = (f32[8,3072]{1,0:T(8,128)}, f32[8,3072]{1,0:T(8,128)S(1)}, u32[]{:S(2)}, u32[]{:S(2)}) collective-permute-start(f32[8,3072]{1,0:T(8,128)} %get-tuple-element.79), channel_id=1, source_target_pairs={{0,24},{1,25},{2,26},{3,27},{4,28},{5,29},{6,30},{7,31},{8,32},{9,... | collective-permute-start | bytes 294920
  1269.9 43.7 %collective-permute-start.88 = (f32[8,3072]{1,0:T(8,128)}, f32[8,3072]{1,0:T(8,128)S(1)}, u32[]{:S(2)}, u32[]{:S(2)}) collective-permute-start(f32[8,3072]{1,0:T(8,128)} %get-tuple-element.79), channel_id=1, source_target_pairs={{0,25},{1,26},{2,27},{3,28},{4,29},{5,30},{6,31},{7,32},{8,33},{9,... | collective-permute-start | bytes 294920
  1271.7 44.4 %collective-permute-start.89 = (f32[8,3072]{1,0:T(8,128)}, f32[8,3072]{1,0:T(8,128)S(1)}, u32[]{:S(2)}, u32[]{:S(2)}) collective-permute-start(f32[8,3072]{1,0:T(8,128)} %get-tuple-element.79), channel_id=1, source_target_pairs={{0,26},{1,27},{2,28},{3,29},{4,30},{5,31},{6,32},{7,33},{8,34},{9,... | collective-permute-start | bytes 294920
  (395 other events, 12643.1 us)
Sparse Core Ops, SparseCore 0:
  10.8 71.4 all-gather.12
  85.1 65.4 all-gather.10
  153.6 67.1 all-gather.14
  223.4 64.3 all-gather.8
  350.7 230.3 reduce-scatter.9
where the time goes:
time: 1400 us; the launch traced here: 1380 us
  blocking collectives  614 us (44%)
  starting transfers between devices  367 us (26%)
  local copies, waits for them, and re-layouts  199 us (14%)
  matrix products  110 us (8%)
  other arithmetic  44.6 us (3%)
  waiting for transfers between devices  23.7 us (2%)
  between operations  19.8 us (1%)
    unnamed x3, blocking collectives  532 us
    unnamed x128, starting transfers between devices  343 us
    unnamed x614, local copies, waits for them, and re-layouts  153 us
    all_gather x1, blocking collectives, on_device(): lax.all_gather(shards[4], ('dp', 'fsdp'), axis=0, tiled=True)  81.8 us
    dot_general x13, matrix products, matmul(): return jnp.dot(left, right, preferred_element_type=jnp.float32)  39 us
    dot_general x11, matrix products, left_t(): lax.dot_general(left, right, (((0,), (0,)), ((), ())), preferred_element_...  31.5 us
  transfers between devices with their start and end apart: 137, of which 2 were waited for; matrix products, arithmetic and copies ran while one was open for 50% of the time, Pallas kernels for 0%

commit v1 on v0

v1 whole, which is shorter than its diff:
```python
import functools

import jax
import jax.numpy as jnp
from jax import lax
from jax.experimental import pallas as pl
from jax.experimental.pallas import tpu as pltpu
from jax.sharding import PartitionSpec as P

MESH = pl.DeviceIdType.MESH
BF, F32, I32 = jnp.bfloat16, jnp.float32, jnp.int32
ROWS, D, FF, DE, HEADS = 512, 768, 3072, 512, 12
PLANE, STRIPS, STRIP_POS, SEG = 16, 8, 529, 128
OUT_ROWS = STRIPS * STRIP_POS
WINDOW = 272
EPS = 1e-06
MASKED = -1e9
H_VEC, H_QKV, H_OUT, H_UP, H_DOWN, H_EMBED = 0, 1, 10, 13, 25, 37
GROUPS = ((0, 2), (2, 3))
ORDERS = ("xyz", "yzx", "zxy")
V_BE, V_MASK = 12, 13


def dot(a, b):
    return jnp.dot(a, b, preferred_element_type=F32)


def dot_t(a, b):
    return lax.dot_general(a, b, (((1,), (1,)), ((), ())), preferred_element_type=F32)


def tdot(a, b):
    return lax.dot_general(a, b, (((0,), (0,)), ((), ())), preferred_element_type=F32)


def iota(shape, dim):
    return lax.broadcasted_iota(I32, shape, dim)


def hot(mask):
    return jnp.where(mask, 1.0, 0.0).astype(BF)


def spread_hot(each, first):
    row, col = iota((D, 256), 0), iota((D, 256), 1) + first
    owner = (col * 10923) >> 16 if each == 6 else col >> 2
    return hot(row == 6 * owner)


class Place:
    def __init__(self):
        self.dp = lax.axis_index("dp")
        self.fs = lax.axis_index("fsdp")
        self.z, self.c = self.dp // 2, self.dp % 2
        self.y, self.x = self.fs // 4, self.fs % 4
        self.own = {"x": self.x, "y": self.y, "z": self.z}

    def near(self, axis, step):
        at = dict(self.own)
        at[axis] = (at[axis] + step) % 4
        return (at["z"] * 2 + self.c, at["y"] * 4 + at["x"])

    def sibling(self):
        return (self.z * 2 + 1 - self.c, self.fs)

    def plane(self, step):
        return (self.dp, (self.fs + step) % PLANE)


def enter(place):
    barrier = pltpu.get_barrier_semaphore()
    others = [place.near("z", s) for s in (1, 2, 3)] + [place.sibling()]
    others += [place.plane(t) for t in range(1, PLANE)]
    for other in others:
        pl.semaphore_signal(barrier, inc=1, device_id=other, device_id_type=MESH)
    pl.semaphore_wait(barrier, len(others))


class Links:
    def __init__(self, send_sem, recv_sem):
        self.send_sem, self.recv_sem = send_sem, recv_sem
        self.used = 0
        self.started = []

    def make(self, src, dst, index, device):
        return pltpu.make_async_remote_copy(
            src_ref=src,
            dst_ref=dst,
            send_sem=self.send_sem.at[index],
            recv_sem=self.recv_sem.at[index],
            device_id=device,
            device_id_type=MESH,
        )

    def send(self, src, dst, device):
        index = self.used
        self.used += 1
        copy = self.make(src, dst, index, device)
        copy.start()
        self.started.append(copy)
        return index

    def arrive(self, dst, index, device):
        self.make(dst, dst, index, device).wait_recv()

    def drain(self):
        for copy in self.started:
            copy.wait_send()
        self.started = []


def region(ks, coords, core, rows):
    ys = slice(None) if coords["y"] is None else coords["y"]
    zs = slice(None) if coords["z"] is None else coords["z"]
    xs = (
        slice(None)
        if coords["x"] is None
        else pl.ds(pl.multiple_of(coords["x"] * 128, 128), 128)
    )
    return (pl.ds(ks[0], ks[1]), ys, zs, core, rows, xs)


def rows_of(part, half=None):
    return pl.ds(32 * part, 32) if half is None else pl.ds(32 * part + 16 * half, 16)


def free(own, order, count):
    return {a: (None if a in order[:count] else own[a]) for a in "xyz"}


class Spread:
    def __init__(self, place, links, g, ks):
        self.p, self.l, self.g, self.ks = place, links, g, ks

    def at(self, coords, part, half=None, core=None):
        core = self.p.c if core is None else core
        return self.g.at[region(self.ks, coords, core, rows_of(part, half))]

    def send(self, coords, part, half, device):
        view = self.at(coords, part, half)
        return self.l.send(view, view, device)

    def direct(self, phase):
        sent = []
        for part, order in enumerate(ORDERS):
            coords = free(self.p.own, order, phase)
            axis = order[phase]
            for step in (1, 3, 2):
                index = self.send(coords, part, None, self.p.near(axis, step))
                sent.append((part, coords, axis, step, index))
        return sent

    def direct_arrive(self, sent):
        for part, coords, axis, step, index in sent:
            source = dict(coords, **{axis: (self.p.own[axis] + 4 - step) % 4})
            self.l.arrive(self.at(source, part), index, self.p.near(axis, 4 - step))

    def one(self):
        self.sent1 = self.direct(0)

    def two(self):
        self.direct_arrive(self.sent1)
        self.sent2 = self.direct(1)

    def three(self):
        self.direct_arrive(self.sent2)
        self.sib = []
        self.sent3 = []
        for part, order in enumerate(ORDERS):
            axis, base = order[2], free(self.p.own, order, 2)
            up = self.send(base, part, None, self.p.near(axis, 1))
            down = self.send(base, part, None, self.p.near(axis, 3))
            self.sent3.append((up, down))
        for part, order in enumerate(ORDERS):
            self.share(free(self.p.own, order, 2), part, None)

    def share(self, coords, part, half):
        index = self.send(coords, part, half, self.p.sibling())
        self.sib.append((coords, part, half, index))

    def four(self):
        self.sent4 = []
        for part, order in enumerate(ORDERS):
            axis, base = order[2], free(self.p.own, order, 2)
            up, down = self.sent3[part]
            own = self.p.own[axis]
            below = dict(base, **{axis: (own + 3) % 4})
            above = dict(base, **{axis: (own + 1) % 4})
            self.l.arrive(self.at(below, part), up, self.p.near(axis, 3))
            go_up = self.send(below, part, 0, self.p.near(axis, 1))
            self.l.arrive(self.at(above, part), down, self.p.near(axis, 1))
            go_down = self.send(above, part, 1, self.p.near(axis, 3))
            self.sent4.append((go_up, go_down))
            self.share(below, part, None)
            self.share(above, part, None)

    def five(self):
        for part, order in enumerate(ORDERS):
            axis, base = order[2], free(self.p.own, order, 2)
            go_up, go_down = self.sent4[part]
            far = dict(base, **{axis: (self.p.own[axis] + 2) % 4})
            self.l.arrive(self.at(far, part, 0), go_up, self.p.near(axis, 3))
            self.share(far, part, 0)
            self.l.arrive(self.at(far, part, 1), go_down, self.p.near(axis, 1))
            self.share(far, part, 1)

    def six(self):
        for coords, part, half, index in self.sib:
            self.l.arrive(
                self.at(coords, part, half, 1 - self.p.c), index, self.p.sibling()
            )


class Gather:
    def __init__(self, place, links, g, ks, bufs):
        self.p, self.l, self.g, self.ks = place, links, g, ks
        self.core_buf, self.half_bufs, self.full_bufs, self.two_bufs, self.one_bufs = bufs

    def at(self, coords, part, half=None):
        return self.g.at[region(self.ks, coords, self.p.c, rows_of(part, half))]

    def k(self):
        return pl.ds(self.ks[0], self.ks[1])

    def add(self, coords, start, count, reads):
        xs = (
            slice(None)
            if coords["x"] is None
            else pl.ds(pl.multiple_of(coords["x"] * 128, 128), 128)
        )

        def body(k, _):
            for y in range(4) if coords["y"] is None else (coords["y"],):
                for z in range(4) if coords["z"] is None else (coords["z"],):
                    place = (k, y, z, self.p.c, pl.ds(start, count), xs)
                    total = self.g[place].astype(F32)
                    for read in reads:
                        total = total + read(k, y, z).astype(F32)
                    self.g[place] = total.astype(BF)
            return 0

        lax.fori_loop(self.ks[0], self.ks[0] + self.ks[1], body, 0)

    @staticmethod
    def reader(buf, coords, slot):
        def read(k, y, z):
            index = (slot, k)
            index += (y,) if coords["y"] is None else ()
            index += (z,) if coords["z"] is None else ()
            return buf[index]

        return read

    def one(self):
        src = self.g.at[self.k(), :, :, 1 - self.p.c]
        self.sent = self.l.send(src, self.core_buf.at[0 : self.ks[1]], self.p.sibling())

    def two(self):
        self.l.arrive(self.core_buf.at[0 : self.ks[1]], self.sent, self.p.sibling())
        whole = {"x": None, "y": None, "z": None}
        self.sent1 = []
        for part, order in enumerate(ORDERS):
            rows = rows_of(part)
            self.add(whole, 32 * part, 32, [lambda k, y, z: self.core_buf[k - self.ks[0], y, z, rows]])
            axis, base = order[2], free(self.p.own, order, 2)
            far = dict(base, **{axis: (self.p.own[axis] + 2) % 4})
            buf = self.half_bufs[part]
            up = self.l.send(self.at(far, part, 0), buf.at[0, self.k()], self.p.near(axis, 1))
            down = self.l.send(self.at(far, part, 1), buf.at[1, self.k()], self.p.near(axis, 3))
            self.sent1.append((up, down))

    def three(self):
        self.sent2 = []
        for part, order in enumerate(ORDERS):
            axis, base = order[2], free(self.p.own, order, 2)
            half, full = self.half_bufs[part], self.full_bufs[part]
            up, down = self.sent1[part]
            above = dict(base, **{axis: (self.p.own[axis] + 1) % 4})
            below = dict(base, **{axis: (self.p.own[axis] + 3) % 4})
            self.l.arrive(half.at[0, self.k()], up, self.p.near(axis, 3))
            self.add(above, 32 * part, 16, [self.reader(half, above, 0)])
            go_up = self.l.send(self.at(above, part), full.at[0, self.k()], self.p.near(axis, 1))
            self.l.arrive(half.at[1, self.k()], down, self.p.near(axis, 1))
            self.add(below, 32 * part + 16, 16, [self.reader(half, below, 1)])
            go_down = self.l.send(
                self.at(below, part), full.at[1, self.k()], self.p.near(axis, 3)
            )
            self.sent2.append((go_up, go_down))

    def direct(self, coords, part, axis, buf):
        sent = []
        for step in (1, 3, 2):
            target = dict(coords, **{axis: (self.p.own[axis] + step) % 4})
            device = self.p.near(axis, step)
            sent.append(
                (step, self.l.send(self.at(target, part), buf.at[step - 1, self.k()], device))
            )
        return sent

    def direct_arrive(self, sent, coords, part, axis, buf):
        for step, index in sent:
            self.l.arrive(buf.at[step - 1, self.k()], index, self.p.near(axis, 4 - step))
        self.add(coords, 32 * part, 32, [self.reader(buf, coords, s) for s in range(3)])

    def four(self):
        self.sent3 = []
        for part, order in enumerate(ORDERS):
            axis, base = order[2], free(self.p.own, order, 2)
            full = self.full_bufs[part]
            up, down = self.sent2[part]
            self.l.arrive(full.at[0, self.k()], up, self.p.near(axis, 3))
            self.l.arrive(full.at[1, self.k()], down, self.p.near(axis, 1))
            self.add(
                base, 32 * part, 32, [self.reader(full, base, 0), self.reader(full, base, 1)]
            )
            coords = free(self.p.own, order, 1)
            self.sent3.append(self.direct(coords, part, order[1], self.two_bufs[part]))

    def five(self):
        self.sent4 = []
        for part, order in enumerate(ORDERS):
            coords = free(self.p.own, order, 1)
            self.direct_arrive(self.sent3[part], coords, part, order[1], self.two_bufs[part])
            self.sent4.append(self.direct(self.p.own, part, order[0], self.one_bufs[part]))

    def six(self):
        for part, order in enumerate(ORDERS):
            self.direct_arrive(
                self.sent4[part], self.p.own, part, order[0], self.one_bufs[part]
            )


def reduce_bufs():
    half = [(2, 5, 4, 16, 512), (2, 5, 4, 4, 16, 128), (2, 5, 4, 16, 512)]
    full = [(2, 5, 4, 32, 512), (2, 5, 4, 4, 32, 128), (2, 5, 4, 32, 512)]
    two = [(3, 5, 32, 512), (3, 5, 4, 32, 128), (3, 5, 4, 32, 128)]
    one = [(3, 5, 32, 128)] * 3
    return [(3, 4, 4, 96, 512)] + half + full + two + one


def mean_rows(v):
    return jnp.mean(v, -1, keepdims=True)


def hat_of(v):
    center = v - mean_rows(v)
    factor = lax.rsqrt(mean_rows(center * center) + EPS)
    return center * factor, factor


def norm_back(dy, gain, hat, factor):
    scaled = dy * gain
    return factor * (scaled - mean_rows(scaled) - hat * mean_rows(scaled * hat))


def col_sum(v):
    return jnp.sum(v, 0, keepdims=True)


SCRATCH = {
    "g": ((5, 4, 4, 2, 96, 512), BF),
    "rb": ((PLANE, 32, 128), BF),
    "fin_send": ((PLANE, 32, 128), BF),
    "fin_recv": ((PLANE, 32, 128), BF),
    "meta_all": ((PLANE, 8, 128), I32),
    "n1": ((ROWS, D), BF),
    "qkv": ((ROWS, 3 * D), BF),
    "prob": ((2 * HEADS, 256, 256), BF),
    "ctx": ((ROWS, D), BF),
    "h1": ((ROWS, D), F32),
    "n2": ((ROWS, D), BF),
    "act": ((ROWS, FF), BF),
    "slope": ((ROWS, FF), BF),
    "hb": ((ROWS, D), BF),
    "low": ((ROWS, D), BF),
    "emb": ((ROWS, DE), BF),
    "wide": ((ROWS, D), F32),
    "acc": ((ROWS, D), F32),
    "vec": ((16, D), F32),
    "vgrad": ((16, D), F32),
    "bqkv": ((8, 3 * D), F32),
    "bup": ((8, FF), F32),
    "dec": ((OUT_ROWS, DE), BF),
    "perm": ((STRIPS, WINDOW, SEG), BF),
    "out_slots": ((PLANE, SEG, DE), BF),
    "in_slots": ((PLANE, SEG, DE), BF),
}
N_SEM = 256


def kernel(shard, meta, x_ref, cot, dec_out, patch_out, fin, *refs):
    s = dict(zip(SCRATCH, refs))
    rest = refs[len(SCRATCH):]
    bufs, (send_sem, recv_sem, local_sem, core_free, slot_free) = rest[:13], rest[13:]
    bufs = (bufs[0], bufs[1:4], bufs[4:7], bufs[7:10], bufs[10:13])
    g = s["g"]
    place = Place()
    links = Links(send_sem, recv_sem)

    def weight(h):
        tile = h // 2
        lanes = pl.ds(pl.multiple_of((h % 2) * 256, 256), 256)
        return g[tile // 4, tile % 4, :, :, :, lanes].reshape(D, 256)

    def put_grad(h, value):
        tile = h // 2
        lanes = pl.ds(pl.multiple_of((h % 2) * 256, 256), 256)
        g[tile // 4, tile % 4, :, :, :, lanes] = value.astype(BF).reshape(4, 2, 96, 256)

    def cols(i, width=256):
        return pl.ds(pl.multiple_of(i * width, width), width)

    cot_load = pltpu.make_async_copy(cot, s["dec"], local_sem.at[0])
    cot_load.start()
    enter(place)
    rb, meta_all = s["rb"], s["meta_all"]
    sent = []
    for t in range(1, PLANE):
        to = place.plane(t)
        sent.append(links.send(shard.at[to[1]], rb.at[place.fs], to))
    meta_sent = []
    for t in range(1, PLANE):
        meta_sent.append(links.send(meta, meta_all.at[place.fs], place.plane(t)))
    rb[place.fs] = shard[place.fs]
    meta_all[place.fs] = meta[...]
    for t in range(1, PLANE):
        source = place.plane(PLANE - t)
        links.arrive(rb.at[source[1]], sent[t - 1], source)
    arrived = rb[...].reshape(PLANE * 32, 128)
    row, col = iota((96, PLANE * 32), 0), iota((96, PLANE * 32), 1)
    sender = (row * 43) >> 8
    target = sender * 32 + (row - sender * 6)
    own_lanes = pl.ds(pl.multiple_of(place.x * 128, 128), 128)
    for k in range(5):
        block = dot(hot(col == target + 6 * k), arrived).astype(BF)
        g[k, place.y, place.z, place.c, :, own_lanes] = block

    spreads = [Spread(place, links, g, ks) for ks in GROUPS]
    first, later = spreads
    first.one()
    later.one()
    first.two()
    later.two()
    first.three()
    later.three()

    for t in range(1, PLANE):
        source = place.plane(PLANE - t)
        links.arrive(meta_all.at[source[1]], meta_sent[t - 1], source)
    cot_load.wait()

    def lens_of(m, blk):
        lens = [m[4:5, blk * 4 + j : blk * 4 + j + 1].astype(F32) for j in range(4)]
        starts = [jnp.zeros_like(lens[0])]
        for j in range(3):
            starts.append(starts[j] + lens[j])
        return lens, starts

    total = jnp.zeros((1, DE), F32)
    orders = [meta[5:6, k : k + 1] for k in range(STRIPS)]
    for k in range(STRIPS):
        m = jnp.zeros((8, 128), I32)
        for source in range(PLANE):
            here = orders[k] == (place.fs + PLANE - source) % PLANE
            m = jnp.where(here, meta_all[source], m)
        blk, j = k // 4, k % 4
        lens, starts = lens_of(m, blk)
        skip = jnp.concatenate([m[2 * blk : 2 * blk + 1], m[2 * blk + 1 : 2 * blk + 2]], 1)
        skip = jnp.broadcast_to(skip.astype(F32), (8, 256)).astype(BF)
        r, t = iota((256, SEG), 0).astype(F32), iota((256, SEG), 1).astype(F32)
        local = dot(skip, hot(r - starts[j] == t))
        tri = hot(iota((SEG, SEG), 0) <= iota((SEG, SEG), 1))
        through = dot(local.astype(BF), tri)[0:1]
        off = (STRIP_POS * k) % 16
        base = STRIP_POS * k - off
        lane = iota((WINDOW, SEG), 1).astype(F32)
        spot = iota((WINDOW, SEG), 0).astype(F32)
        perm = hot((spot == lane + through + float(off)) & (lane < lens[j]))
        s["perm"][k] = perm
        picked = tdot(perm, s["dec"][base : base + WINDOW])
        s["act"][SEG * j : SEG * j + SEG, DE * blk : DE * blk + DE] = picked.astype(BF)
        total = total - col_sum(picked)

    def sum_rows(i, acc):
        part = s["dec"][pl.ds(pl.multiple_of(i * 16, 16), 16), :].astype(F32)
        return acc + part

    summed = lax.fori_loop(0, OUT_ROWS // 16, sum_rows, jnp.zeros((16, DE), F32))
    total = total + col_sum(summed) + col_sum(s["dec"][OUT_ROWS - 8 :, :].astype(F32))
    s["vgrad"][...] = jnp.zeros_like(s["vgrad"])
    s["vgrad"][V_MASK : V_MASK + 1, 0:DE] = total

    def weight_of(k, value):
        return jnp.where(orders[k] == value, 1.0, 0.0).astype(BF)

    def fill_slot(t, _):
        total = jnp.zeros((SEG, DE), BF)
        for k in range(STRIPS):
            blk, j = k // 4, k % 4
            one = s["act"][SEG * j : SEG * j + SEG, DE * blk : DE * blk + DE]
            total = total + one * weight_of(k, (PLANE - t) % PLANE)
        s["out_slots"][t] = total
        return 0

    lax.fori_loop(0, PLANE, fill_slot, 0)

    first.four()
    later.four()
    first.five()
    first.six()
    later.five()
    later.six()
    cot_sent = []
    for t in range(1, PLANE):
        cot_sent.append(
            links.send(s["out_slots"].at[t], s["in_slots"].at[t], place.plane(t))
        )
    s["in_slots"][0] = s["out_slots"][0]

    chunk = g[0, 0, :, :, :, 0:128].reshape(D, 128)
    table = s["acc"]

    def spread_six(i, _):
        table[0:128, cols(i)] = tdot(chunk, spread_hot(6, 256 * i))
        return 0

    def spread_four(i, _):
        table[128:256, cols(i)] = tdot(chunk, spread_hot(4, 256 * i))
        return 0

    lax.fori_loop(0, 3, spread_six, 0)
    lax.fori_loop(0, 2, spread_four, 0)
    lane6 = iota((16, D), 1)
    lane6 = lane6 - 6 * ((lane6 * 10923) >> 16)
    row6 = iota((16, D), 0)
    for v in range(12):
        low = (6 * v) // 8 * 8
        window = table[low : low + 16, :]
        s["vec"][v : v + 1] = col_sum(jnp.where(row6 + (low - 6 * v) == lane6, window, 0.0))
    lane4, row4 = iota((8, DE), 1) & 3, iota((8, DE), 0)
    few = table[128 + 72 : 128 + 80, 0:DE]
    for i, v in enumerate((V_BE, V_MASK)):
        s["vec"][v : v + 1, 0:DE] = col_sum(jnp.where(row4 - 4 * i == lane4, few, 0.0))
    vec = s["vec"]
    s["bqkv"][...] = jnp.zeros_like(s["bqkv"])
    s["bqkv"][0:1, 0:D] = vec[4:5]
    s["bqkv"][0:1, 2 * D :] = vec[5:6]
    for q in range(4):
        s["bup"][0:1, q * D : (q + 1) * D] = vec[8 + q : 9 + q]

    def norm_one(i, _):
        rows = cols(i, 128)
        hat, _f = hat_of(x_ref[rows, :].astype(F32))
        s["n1"][rows, :] = (hat * vec[0:1] + vec[1:2]).astype(BF)
        return 0

    lax.fori_loop(0, 4, norm_one, 0)

    def qkv_tile(t, _):
        for i in range(2):
            rows = cols(i)
            out = dot(s["n1"][rows, :], weight(H_QKV + t)) + s["bqkv"][0:1, cols(t)]
            s["qkv"][rows, cols(t)] = out.astype(BF)
        return 0

    lax.fori_loop(0, 9, qkv_tile, 0)

    lens_own = [lens_of(meta[...], b) for b in range(2)]

    def doc_bias(starts):
        r, c = iota((256, 256), 0).astype(F32), iota((256, 256), 1).astype(F32)
        doc_r, doc_c = jnp.zeros_like(r), jnp.zeros_like(c)
        for j in range(1, 4):
            doc_r = doc_r + jnp.where(r >= starts[j], 1.0, 0.0)
            doc_c = doc_c + jnp.where(c >= starts[j], 1.0, 0.0)
        return doc_r == doc_c

    lane = iota((256, 128), 1)
    for blk in range(2):
        rows = slice(256 * blk, 256 * blk + 256)
        same = doc_bias(lens_own[blk][1])

        def heads(hp, _):
            q2 = s["qkv"][rows, cols(hp, 128)] * jnp.asarray(0.125, BF)
            k2 = s["qkv"][rows, cols(6 + hp, 128)]
            v2 = s["qkv"][rows, cols(12 + hp, 128)]
            outs = []
            for h in range(2):
                mine = (lane >= 64) if h else (lane < 64)
                scores = dot_t(jnp.where(mine, q2, jnp.zeros_like(q2)), k2)
                scores = jnp.where(same, scores, MASKED)
                e = jnp.exp(scores - jnp.max(scores, -1, keepdims=True))
                p = (e * (1.0 / jnp.sum(e, -1, keepdims=True))).astype(BF)
                s["prob"][12 * blk + 2 * hp + h] = p
                outs.append(dot(p, v2))
            s["ctx"][rows, cols(hp, 128)] = jnp.where(lane < 64, outs[0], outs[1]).astype(BF)
            return 0

        lax.fori_loop(0, 6, heads, 0)

    def out_tile(t, _):
        out = dot(s["ctx"][...], weight(H_OUT + t)) + vec[6:7, cols(t)]
        s["h1"][:, cols(t)] = x_ref[:, cols(t)].astype(F32) + out
        return 0

    lax.fori_loop(0, 3, out_tile, 0)

    def norm_two(i, _):
        rows = cols(i, 128)
        hat, _f = hat_of(s["h1"][rows, :])
        s["n2"][rows, :] = (hat * vec[2:3] + vec[3:4]).astype(BF)
        return 0

    lax.fori_loop(0, 4, norm_two, 0)

    def up_tile(t, _):
        for i in range(2):
            rows = cols(i)
            u = dot(s["n2"][rows, :], weight(H_UP + t)) + s["bup"][0:1, cols(t)]
            phi = 0.5 * (1.0 + lax.erf(u * 0.7071067811865476))
            density = jnp.exp(-0.5 * u * u) * 0.3989422804014327
            s["act"][rows, cols(t)] = (u * phi).astype(BF)
            s["slope"][rows, cols(t)] = (phi + u * density).astype(BF)
        return 0

    lax.fori_loop(0, 12, up_tile, 0)
    for t in range(3):
        for i in range(2):
            rows = cols(i)
            out = s["h1"][rows, cols(t)] + vec[7:8, cols(t)]
            for q in range(4):
                out = out + dot(s["act"][rows, cols(q, D)], weight(H_DOWN + 3 * q + t))
            s["hb"][rows, cols(t)] = out.astype(BF)
    for t in range(2):
        out = dot(s["hb"][...], weight(H_EMBED + t)) + vec[V_BE : V_BE + 1, cols(t)]
        s["emb"][:, cols(t)] = out.astype(BF)

    slot = iota((1, PLANE), 1)
    slot_start, slot_len = jnp.zeros((1, PLANE), F32), jnp.zeros((1, PLANE), F32)
    for k in range(STRIPS):
        blk, j = k // 4, k % 4
        lens, starts = lens_own[blk]
        slot_start = jnp.where(orders[k] == slot, starts[j] + 256.0 * blk, slot_start)
        slot_len = jnp.where(orders[k] == slot, lens[j], slot_len)

    def slot_hot(t):
        i, r = iota((SEG, ROWS), 0).astype(F32), iota((SEG, ROWS), 1).astype(F32)
        start, size = slot_start[:, t : t + 1], slot_len[:, t : t + 1]
        return hot((r - start == i) & (i < size))

    for t in range(1, PLANE):
        links.arrive(s["in_slots"].at[t], cot_sent[t - 1], place.plane(PLANE - t))
    de = s["emb"]
    total = jnp.zeros((ROWS, DE), F32)
    links.drain()
    for t in range(PLANE):
        pick = slot_hot(t)
        total = total + tdot(pick, s["in_slots"][(PLANE - t) % PLANE])
        s["out_slots"][t] = dot(pick, s["emb"][...]).astype(BF)
    de[...] = total.astype(BF)
    for t in range(1, PLANE):
        pl.semaphore_signal(slot_free, inc=1, device_id=place.plane(t), device_id_type=MESH)
    pl.semaphore_wait(slot_free, PLANE - 1)
    emb_sent = []
    for t in range(1, PLANE):
        emb_sent.append(
            links.send(s["out_slots"].at[t], s["in_slots"].at[t], place.plane(t))
        )
    s["in_slots"][0] = s["out_slots"][0]

    vg = s["vgrad"]
    vg[V_BE : V_BE + 1, 0:DE] = col_sum(de[...].astype(F32))
    wide = s["wide"]

    def embed_back(i, acc):
        rows = cols(i)
        dh = dot_t(de[rows, 0:256], weight(H_EMBED)) + dot_t(de[rows, 256:], weight(H_EMBED + 1))
        wide[rows, :] = dh
        s["low"][rows, :] = dh.astype(BF)
        return acc + col_sum(dh)

    vg[7:8] = lax.fori_loop(0, 2, embed_back, jnp.zeros((1, D), F32))
    for t in range(2):
        put_grad(H_EMBED + t, tdot(s["hb"][...], de[:, cols(t)]))

    def down_part(q, _):

        def rows_part(i, acc):
            rows = cols(i)
            da = dot_t(s["low"][rows, 0:256], weight(H_DOWN + 3 * q))
            for t in range(1, 3):
                da = da + dot_t(s["low"][rows, cols(t)], weight(H_DOWN + 3 * q + t))
            du = (da * s["slope"][rows, cols(q, D)].astype(F32)).astype(BF)
            s["slope"][rows, cols(q, D)] = du
            return acc + col_sum(du.astype(F32))

        vg[pl.ds(8 + q, 1), :] = lax.fori_loop(0, 2, rows_part, jnp.zeros((1, D), F32))
        a = s["act"][:, cols(q, D)]
        for t in range(3):
            put_grad(H_DOWN + 3 * q + t, tdot(a, s["low"][:, cols(t)]))
        return 0

    lax.fori_loop(0, 4, down_part, 0)
    acc = s["acc"]

    def up_part(q, _):
        def rows_part(i, _):
            rows = cols(i)
            total = dot_t(s["slope"][rows, cols(3 * q)], weight(H_UP + 3 * q))
            for t in range(1, 3):
                total = total + dot_t(s["slope"][rows, cols(3 * q + t)], weight(H_UP + 3 * q + t))
            acc[rows, :] = jnp.where(q == 0, total, acc[rows, :] + total)
            return 0

        lax.fori_loop(0, 2, rows_part, 0)
        for t in range(3):
            put_grad(H_UP + 3 * q + t, tdot(s["n2"][...], s["slope"][:, cols(3 * q + t)]))
        return 0

    lax.fori_loop(0, 4, up_part, 0)

    def norm_two_back(i, sums):
        rows = cols(i, 128)
        hat, factor = hat_of(s["h1"][rows, :])
        dn = acc[rows, :]
        dh = wide[rows, :] + norm_back(dn, vec[2:3], hat, factor)
        wide[rows, :] = dh
        s["low"][rows, :] = dh.astype(BF)
        return (sums[0] + col_sum(dn * hat), sums[1] + col_sum(dn), sums[2] + col_sum(dh))

    zero = jnp.zeros((1, D), F32)
    vg[2:3], vg[3:4], vg[6:7] = lax.fori_loop(0, 4, norm_two_back, (zero, zero, zero))

    gathers = [Gather(place, links, g, ks, bufs) for ks in GROUPS]
    g_first, g_later = gathers

    def out_back(i, _):
        rows = cols(i)
        total = dot_t(s["low"][rows, 0:256], weight(H_OUT))
        for t in range(1, 3):
            total = total + dot_t(s["low"][rows, cols(t)], weight(H_OUT + t))
        s["hb"][rows, :] = total.astype(BF)
        return 0

    lax.fori_loop(0, 2, out_back, 0)
    for t in range(3):
        put_grad(H_OUT + t, tdot(s["ctx"][...], s["low"][:, cols(t)]))

    for blk in range(2):
        rows = slice(256 * blk, 256 * blk + 256)

        def heads_back(hp, _):
            q2 = s["qkv"][rows, cols(hp, 128)]
            k2 = s["qkv"][rows, cols(6 + hp, 128)]
            v2 = s["qkv"][rows, cols(12 + hp, 128)]
            do2 = s["hb"][rows, cols(hp, 128)]
            dq, dk, dv = [], [], []
            for h in range(2):
                mine = (lane >= 64) if h else (lane < 64)
                p = s["prob"][12 * blk + 2 * hp + h]
                dp = dot_t(jnp.where(mine, do2, jnp.zeros_like(do2)), v2)
                pf = p.astype(F32)
                inner = jnp.sum(pf * dp, -1, keepdims=True)
                ds = (pf * (dp - inner)).astype(BF)
                dq.append(dot(ds, k2))
                dk.append(tdot(ds, q2))
                dv.append(tdot(p, do2))
            lo = lane < 64
            s["qkv"][rows, cols(hp, 128)] = (jnp.where(lo, dq[0], dq[1]) * 0.125).astype(BF)
            s["qkv"][rows, cols(6 + hp, 128)] = (jnp.where(lo, dk[0], dk[1]) * 0.125).astype(BF)
            s["qkv"][rows, cols(12 + hp, 128)] = jnp.where(lo, dv[0], dv[1]).astype(BF)
            return 0

        lax.fori_loop(0, 6, heads_back, 0)

    def bias_sums(i, sums):
        rows = cols(i, 64)
        q = s["qkv"][rows, 0:D].astype(F32)
        v = s["qkv"][rows, 2 * D :].astype(F32)
        return (sums[0] + col_sum(q), sums[1] + col_sum(v))

    vg[4:5], vg[5:6] = lax.fori_loop(0, 8, bias_sums, (zero, zero))

    def qkv_part(q, _):
        def rows_part(i, _):
            rows = cols(i)
            total = dot_t(s["qkv"][rows, cols(3 * q)], weight(H_QKV + 3 * q))
            for t in range(1, 3):
                total = total + dot_t(s["qkv"][rows, cols(3 * q + t)], weight(H_QKV + 3 * q + t))
            acc[rows, :] = jnp.where(q == 0, total, acc[rows, :] + total)
            return 0

        lax.fori_loop(0, 2, rows_part, 0)
        for t in range(3):
            put_grad(H_QKV + 3 * q + t, tdot(s["n1"][...], s["qkv"][:, cols(3 * q + t)]))
        return 0

    lax.fori_loop(0, 3, qkv_part, 0)

    def norm_one_back(i, sums):
        rows = cols(i, 128)
        hat, factor = hat_of(x_ref[rows, :].astype(F32))
        dn = acc[rows, :]
        wide[rows, :] = wide[rows, :] + norm_back(dn, vec[0:1], hat, factor)
        return (sums[0] + col_sum(dn * hat), sums[1] + col_sum(dn))

    vg[0:1], vg[1:2] = lax.fori_loop(0, 4, norm_one_back, (zero, zero))
    patch_store = pltpu.make_async_copy(wide, patch_out, local_sem.at[1])
    patch_store.start()

    table[0:256, :] = jnp.zeros((256, D), F32)
    lane6 = iota((8, D), 1)
    lane6 = lane6 - 6 * ((lane6 * 10923) >> 16)
    row6 = iota((8, D), 0)
    for a in range(9):
        rows = jnp.zeros((8, D), F32)
        for v in range(12):
            if 6 * v < 8 * a + 8 and 6 * v + 6 > 8 * a:
                rows = jnp.where(row6 + (8 * a - 6 * v) == lane6, vg[v : v + 1], rows)
        table[8 * a : 8 * a + 8, :] = rows
    rows = jnp.zeros((8, DE), F32)
    for i, v in enumerate((V_BE, V_MASK)):
        rows = jnp.where(row4 - 4 * i == lane4, vg[v : v + 1, 0:DE], rows)
    table[128 + 72 : 128 + 80, 0:DE] = rows

    def fold_six(i, total):
        return total + dot_t(spread_hot(6, 256 * i), table[0:128, cols(i)].astype(BF))

    def fold_four(i, total):
        return total + dot_t(spread_hot(4, 256 * i), table[128:256, cols(i)].astype(BF))

    chunk = lax.fori_loop(0, 3, fold_six, jnp.zeros((D, 128), F32))
    chunk = lax.fori_loop(0, 2, fold_four, chunk)
    g[0, 0, :, :, :, 0:128] = chunk.astype(BF).reshape(4, 2, 96, 128)

    g_later.one()
    g_later.two()
    pl.semaphore_signal(core_free, inc=1, device_id=place.sibling(), device_id_type=MESH)
    pl.semaphore_wait(core_free, 1)
    g_first.one()
    g_first.two()
    for t in range(1, PLANE):
        links.arrive(s["in_slots"].at[t], emb_sent[t - 1], place.plane(PLANE - t))
    mask = vec[V_MASK : V_MASK + 1, 0:DE]
    blank = jnp.broadcast_to(mask.astype(BF), (16, DE))

    def fill(i, _):
        s["dec"][cols(i, 16), :] = blank
        return 0

    lax.fori_loop(0, OUT_ROWS // 16, fill, 0)
    s["dec"][OUT_ROWS - 8 :, :] = blank[0:8]
    for k in range(STRIPS):
        perm = s["perm"][k]
        base = STRIP_POS * k - (STRIP_POS * k) % 16

        def find(t, total):
            return total + s["in_slots"][t] * weight_of(k, t)

        strip = lax.fori_loop(0, PLANE, find, jnp.zeros((SEG, DE), BF))
        placed = dot(perm, strip)
        filled = jnp.sum(perm.astype(F32), -1, keepdims=True)
        s["dec"][base : base + WINDOW] = jnp.where(filled > 0.5, placed, mask).astype(BF)
    dec_store = pltpu.make_async_copy(s["dec"], dec_out, local_sem.at[0])
    dec_store.start()
    g_later.three()
    g_first.three()
    g_later.four()
    g_first.four()
    g_later.five()
    g_first.five()
    g_later.six()
    g_first.six()
    row, col = iota((PLANE * 32, 96), 0), iota((PLANE * 32, 96), 1)
    inner_row = row & 31
    base_row = 6 * (row >> 5)
    slots = jnp.zeros((PLANE * 32, 128), F32)
    for k in range(5):
        j = inner_row - 6 * k
        pick = hot((col == base_row + j) & (j >= 0) & (j < 6))
        slots = slots + dot(pick, g[k, place.y, place.z, place.c, :, own_lanes])
    s["fin_send"][...] = slots.astype(BF).reshape(PLANE, 32, 128)
    fin_sent = []
    for t in range(1, PLANE):
        to = place.plane(t)
        fin_sent.append(links.send(s["fin_send"].at[to[1]], s["fin_recv"].at[place.fs], to))
    s["fin_recv"][place.fs] = s["fin_send"][place.fs]
    for t in range(1, PLANE):
        source = place.plane(PLANE - t)
        links.arrive(s["fin_recv"].at[source[1]], fin_sent[t - 1], source)
    fin[...] = s["fin_recv"][...]
    links.drain()
    dec_store.wait()
    patch_store.wait()


def mega(shard, meta, x, cot):
    dma = pltpu.SemaphoreType.DMA
    vmem = pl.BlockSpec(memory_space=pltpu.VMEM)
    hbm = pl.BlockSpec(memory_space=pl.ANY)
    return pl.pallas_call(
        kernel,
        out_shape=(
            jax.ShapeDtypeStruct((OUT_ROWS, DE), BF),
            jax.ShapeDtypeStruct((ROWS, D), F32),
            jax.ShapeDtypeStruct((PLANE, 32, 128), BF),
        ),
        in_specs=[vmem, vmem, vmem, hbm],
        out_specs=(hbm, hbm, vmem),
        scratch_shapes=[pltpu.VMEM(shape, kind) for shape, kind in SCRATCH.values()]
        + [pltpu.VMEM(shape, BF) for shape in reduce_bufs()]
        + [dma((N_SEM,)), dma((N_SEM,)), dma((2,)), pltpu.SemaphoreType.REGULAR, pltpu.SemaphoreType.REGULAR],
        compiler_params=pltpu.CompilerParams(
            collective_id=1, has_side_effects=True, vmem_limit_bytes=64 * 1024 * 1024
        ),
        name="layer",
    )(shard, meta, x, cot)


def on_device(patches, lengths, skipped, strip_order, decoder_grad, qkv_weight, out_weight,
              up_weight, down_weight, embed_weight, gain_one, shift_one, gain_two, shift_two,
              bias_query, bias_value, bias_out, bias_up, bias_down, bias_embed, mask_token):
    vectors = jnp.concatenate(
        [gain_one, shift_one, gain_two, shift_two, bias_query, bias_value, bias_out, bias_down,
         bias_up, bias_embed, mask_token]
    )
    up = up_weight.reshape(6, 128, 4, 6).transpose(0, 2, 1, 3).reshape(6, FF)
    down = down_weight.reshape(4, 6, D).transpose(1, 0, 2).reshape(6, FF)
    first = jnp.zeros((6, 256), BF).at[0, 0:80].set(vectors)
    last = jnp.zeros((6, 256), BF)
    lanes = jnp.concatenate([first, qkv_weight, out_weight, up, down, embed_weight, last], 1)
    shard = lanes.reshape(6, 5, PLANE, 128).transpose(2, 1, 0, 3).reshape(PLANE, 30, 128)
    shard = jnp.pad(shard, ((0, 0), (0, 2), (0, 0)))
    meta = jnp.concatenate(
        [
            skipped.reshape(4, 128),
            jnp.pad(lengths.reshape(1, 8), ((0, 0), (0, 120))),
            jnp.pad(strip_order, ((0, 2), (0, 112))),
        ],
        0,
    )
    dec, patch_grad, fin = mega(shard, meta, patches, decoder_grad)
    fin = fin[:, 0:30].reshape(PLANE, 5, 6, 128).transpose(2, 1, 0, 3).reshape(6, 10240)
    fin = fin.astype(F32)
    parts = []
    at = 256
    for width in (3 * D, D, FF, FF, DE):
        parts.append(fin[:, at : at + width])
        at += width
    g_qkv, g_out, g_up, g_down, g_embed = parts
    g_up = g_up.reshape(6, 4, 128, 6).transpose(0, 2, 1, 3).reshape(6, FF)
    g_down = g_down.reshape(6, 4, D).transpose(1, 0, 2).reshape(24, D)
    v = fin[0, 0:80]
    return (dec, patch_grad, g_qkv, g_out, g_up, g_down, g_embed, v[0:6], v[6:12], v[12:18],
            v[18:24], v[24:30], v[30:36], v[36:42], v[48:72], v[42:48], v[72:76], v[76:80])


def solution(mesh):
    both = ("dp", "fsdp")
    rows, vector = P(both, None), P(both)
    return jax.shard_map(
        on_device,
        mesh=mesh,
        in_specs=(rows, rows, rows, P("dp", None), rows) + (rows,) * 5 + (vector,) * 11,
        out_specs=(rows,) * 7 + (vector,) * 11,
        check_vma=False,
    )
```

time: 1400 us -> 237 us (0.17); the launches traced: 1380 us -> 237 us
  blocking collectives: 614 us -> 0 us
  starting transfers between devices: 367 us -> 0 us
  Pallas kernels: 0 us -> 204 us
  local copies, waits for them, and re-layouts: 199 us -> 30 us
  matrix products: 110 us -> 0 us
  other arithmetic: 44.6 us -> 2.22 us
  waiting for transfers between devices: 23.7 us -> 0 us
  between operations: 19.8 us -> 0.8 us
    unnamed x3 -> x0, blocking collectives: 532 us -> none
    unnamed x128 -> x0, starting transfers between devices: 343 us -> none
    pallas_call x0 -> x1, Pallas kernels: none -> 204 us  [mega(): pl.pallas_call(kernel, out_shape=(jax.ShapeDtypeStruct((OUT_ROWS, DE), BF...]
    unnamed x614 -> x13, local copies, waits for them, and re-layouts: 153 us -> 7.42 us
    dot_general x46 -> x0, matrix products: 110 us -> none  [the longest x13 39 us: matmul(): return jnp.dot(left, right, preferred_element_type=jnp.float32)]
    all_gather x1 -> x0, blocking collectives: 81.8 us -> none  [on_device(): lax.all_gather(shards[4], ('dp', 'fsdp'), axis=0, tiled=True)]
    all_to_all x4 -> x0, starting transfers between devices: 23.4 us -> none  [the longest x1 7.21 us: on_device(): lax.all_to_all(low_sent, 'fsdp', split_axis=0, concat_axis=0, tiled=True)]
    scatter x2 -> x0, local copies, waits for them, and re-layouts: 21 us -> none  [the longest x1 12.7 us: on_device(): placed = jnp.zeros((total_slots, arrived.shape[2]), jnp.bfloat16).at[plac...]
  transfers between devices with their start and end apart: 137 -> 0, of which waited for: 2 -> 0; matrix products, arithmetic and copies ran while one was open for 50% -> 0% of each run, Pallas kernels for 0% -> 0%
where the time goes in v1:
time: 237 us
  Pallas kernels  204 us (86%)
  local copies, waits for them, and re-layouts  30 us (13%)
    pallas_call x1, Pallas kernels, mega(): pl.pallas_call(kernel, out_shape=(jax.ShapeDtypeStruct((OUT_ROWS, DE), BF...  204 us
    concatenate x1, local copies, waits for them, and re-layouts, on_device(): jnp.concatenate([gain_one, shift_one, gain_two, shift_two, bias_query, bi...  7.43 us
    unnamed x13, local copies, waits for them, and re-layouts  7.42 us

profile of v1, /device:TPU:0, one launch (start us, length us, event | category | flops | bytes accessed | tf_op | source)
XLA Modules:
  0.0 236.9 jit_solution(2501513884757340735)
XLA Ops:
  0.7 0.8 reshape.127
  1.4 7.4 %concatenate.11 = bf16[80]{0:T(256)(128)(2,1)S(1)} concatenate(bf16[6]{0:T(256)(128)(2,1)} %param.33, bf16[6]{0:T(256)(128)(2,1)} %param.34, bf16[6]{0:T(256)(128)(2,1)} %param.35, bf16[6]{0:T(256)(128)(2,1)} %param.36, bf16[6]{0:T(256)(128)(2,1)} %param.37, bf16[6]{0:T(256)(128)(2,1)} %param.38, bf16[6]{0:T(256)(128)(2,1)} %param.39, bf16[6]{0:T(256)(128)(2,1)} %param.41, ...), dimensions={0} | concatenate | bytes 320 | tf_op jit(solution)/shard_map/concatenate | solution.py:923
  8.8 1.3 pad_add_fusion.meta
  10.1 0.8 reshape.122
  10.9 0.8 constant_dynamic-update-slice_fusion.5
  11.7 0.7 constant_dynamic-update-slice_fusion.4
  12.4 2.5 %reshape.120 = bf16[6,128,4,6]{3,2,1,0:T(4,128)(2,1)S(1)} reshape(bf16[6,3072]{1,0:T(8,128)(2,1)} %param.30) | data formatting | bytes 73728 | tf_op jit(solution)/shard_map/reshape | solution.py:927
  15.0 0.2 copy.55
  15.2 1.1 reshape.121
  16.4 0.7 pad.17.shard
  17.0 203.8 %layer.1 = (bf16[4232,512]{1,0:T(8,128)(2,1)}, f32[512,768]{1,0:T(8,128)}, bf16[16,32,128]{2,1,0:T(8,128)(2,1)}) custom-call(bf16[16,32,128]{2,1,0:T(8,128)(2,1)} %pad.17.shard, s32[8,128]{1,0:T(8,128)} %pad_add_fusion.meta, bf16[512,768]{1,0:T(8,128)(2,1)} %x_ref.1, bf16[4232,512]{1,0:T(8,128)(2,1)} %cot.1), custom_call_target="tpu_custom_call" | custom-call | tf_op jit(solution)/shard_map/layer/pallas_call | solution.py:901
  220.9 0.9 slice_convert_fusion
  222.1 0.6 slice_bitcast_fusion.3
  222.7 0.6 slice_bitcast_fusion
  223.2 0.6 slice_bitcast_fusion.2
  223.8 0.6 slice.144
  224.5 0.6 slice.141
  225.1 0.6 slice.140
  225.7 0.6 reshape.131
  226.4 1.6 reshape.128
  227.9 1.0 copy.60
  229.0 2.1 reshape.129
  231.0 4.7 %copy.75 = bf16[4232,512]{1,0:T(8,128)(2,1)} copy(bf16[4232,512]{1,0:T(8,128)(2,1)} %get-tuple-element.66) | data formatting | bytes 8667136
  235.7 1.1 copy.76
  (15 shorter events, 0.3 us)
Async XLA Ops:
  12.4 3.8 %copy-start.1 = (bf16[6,512]{1,0:T(8,128)(2,1)S(1)}, bf16[6,512]{1,0:T(8,128)(2,1)}, u32[]{:S(2)}) copy-start(bf16[6,512]{1,0:T(8,128)(2,1)} %param.32) | copy-start | bytes 18436
  231.0 4.7 %copy-start = (f32[512,768]{1,0:T(8,128)S(1)}, f32[512,768]{1,0:T(8,128)}, u32[]{:S(2)}) copy-start(f32[512,768]{1,0:T(8,128)} %get-tuple-element.67) | copy-start | bytes 4718596

commit v2 on v1

--- a/solution.py
+++ b/solution.py
@@ -17,8 +17,10 @@
 MASKED = -1e9
 H_VEC, H_QKV, H_OUT, H_UP, H_DOWN, H_EMBED = 0, 1, 10, 13, 25, 37
 GROUPS = ((0, 2), (2, 3))
+SUM_GROUPS = ((0, 1), (1, 1), (2, 3))
 ORDERS = ("xyz", "yzx", "zxy")
 V_BE, V_MASK = 12, 13
+L_QKV, L_OUT, L_UP, L_DOWN, L_EMBED = 256, 2560, 3328, 6400, 9472
 
 
 def dot(a, b):
@@ -67,13 +69,13 @@
         return (self.dp, (self.fs + step) % PLANE)
 
 
-def enter(place):
+def announce(place):
     barrier = pltpu.get_barrier_semaphore()
     others = [place.near("z", s) for s in (1, 2, 3)] + [place.sibling()]
     others += [place.plane(t) for t in range(1, PLANE)]
     for other in others:
         pl.semaphore_signal(barrier, inc=1, device_id=other, device_id_type=MESH)
-    pl.semaphore_wait(barrier, len(others))
+    return len(others)
 
 
 class Links:
@@ -103,10 +105,11 @@
     def arrive(self, dst, index, device):
         self.make(dst, dst, index, device).wait_recv()
 
-    def drain(self):
-        for copy in self.started:
+    def drain(self, count=None):
+        count = len(self.started) if count is None else count
+        for copy in self.started[:count]:
             copy.wait_send()
-        self.started = []
+        self.started = self.started[count:]
 
 
 def region(ks, coords, core, rows):
@@ -214,6 +217,7 @@
 class Gather:
     def __init__(self, place, links, g, ks, bufs):
         self.p, self.l, self.g, self.ks = place, links, g, ks
+        self.core_first = 0
         self.core_buf, self.half_bufs, self.full_bufs, self.two_bufs, self.one_bufs = bufs
 
     def at(self, coords, part, half=None):
@@ -221,6 +225,9 @@
 
     def k(self):
         return pl.ds(self.ks[0], self.ks[1])
+
+    def core_at(self):
+        return self.core_buf.at[pl.ds(self.core_first, self.ks[1])]
 
     def add(self, coords, start, count, reads):
         xs = (
@@ -251,17 +258,21 @@
 
         return read
 
+    def core_reader(self, rows):
+        shift = self.core_first - self.ks[0]
+        return lambda k, y, z: self.core_buf[k + shift, y, z, rows]
+
     def one(self):
         src = self.g.at[self.k(), :, :, 1 - self.p.c]
-        self.sent = self.l.send(src, self.core_buf.at[0 : self.ks[1]], self.p.sibling())
+        self.sent = self.l.send(src, self.core_at(), self.p.sibling())
 
     def two(self):
-        self.l.arrive(self.core_buf.at[0 : self.ks[1]], self.sent, self.p.sibling())
+        self.l.arrive(self.core_at(), self.sent, self.p.sibling())
         whole = {"x": None, "y": None, "z": None}
         self.sent1 = []
         for part, order in enumerate(ORDERS):
             rows = rows_of(part)
-            self.add(whole, 32 * part, 32, [lambda k, y, z: self.core_buf[k - self.ks[0], y, z, rows]])
+            self.add(whole, 32 * part, 32, [self.core_reader(rows)])
             axis, base = order[2], free(self.p.own, order, 2)
             far = dict(base, **{axis: (self.p.own[axis] + 2) % 4})
             buf = self.half_bufs[part]
@@ -361,7 +372,12 @@
     "g": ((5, 4, 4, 2, 96, 512), BF),
     "rb": ((PLANE, 32, 128), BF),
     "fin_send": ((PLANE, 32, 128), BF),
-    "fin_recv": ((PLANE, 32, 128), BF),
+    "fin_recv": ((32, 2048), BF),
+    "lanes": ((16, 10240), BF),
+    "shard": ((32, 2048), BF),
+    "up16": ((16, FF), BF),
+    "meta": ((8, 128), I32),
+    "strip": ((STRIPS + 1, SEG, DE), BF),
     "meta_all": ((PLANE, 8, 128), I32),
     "n1": ((ROWS, D), BF),
     "qkv": ((ROWS, 3 * D), BF),
@@ -381,17 +397,18 @@
     "bqkv": ((8, 3 * D), F32),
     "bup": ((8, FF), F32),
     "dec": ((OUT_ROWS, DE), BF),
-    "perm": ((STRIPS, WINDOW, SEG), BF),
-    "out_slots": ((PLANE, SEG, DE), BF),
-    "in_slots": ((PLANE, SEG, DE), BF),
+    "slots": ((PLANE, SEG, DE), BF),
 }
-N_SEM = 256
-
-
-def kernel(shard, meta, x_ref, cot, dec_out, patch_out, fin, *refs):
+N_SEM = 260
+
+
+def kernel(
+    w_qkv, w_out, w_up, w_down, w_embed, vectors, skipped, lengths, route, x_ref, cot,
+    patch_out, fin, perms, vec_out, cot_from, cot_to, emb_from, emb_to, *refs
+):
     s = dict(zip(SCRATCH, refs))
     rest = refs[len(SCRATCH):]
-    bufs, (send_sem, recv_sem, local_sem, core_free, slot_free) = rest[:13], rest[13:]
+    bufs, (send_sem, recv_sem, local_sem, core_free) = rest[:13], rest[13:]
     bufs = (bufs[0], bufs[1:4], bufs[4:7], bufs[7:10], bufs[10:13])
     g = s["g"]
     place = Place()
@@ -412,17 +429,53 @@
 
     cot_load = pltpu.make_async_copy(cot, s["dec"], local_sem.at[0])
     cot_load.start()
-    enter(place)
+    callers = announce(place)
+    meta = s["meta"]
+    meta[...] = jnp.zeros_like(meta)
+    meta[0:4, :] = skipped[...]
+    for b in range(2):
+        meta[4:5, 4 * b : 4 * b + 4] = lengths[b : b + 1, :]
+    lanes = s["lanes"]
+    lanes[...] = jnp.zeros_like(lanes)
+    lanes[0:1, 0:128] = vectors[...]
+    lanes[0:6, L_QKV:L_OUT] = w_qkv[...]
+    lanes[0:6, L_OUT:L_UP] = w_out[...]
+    for q in range(4):
+        lanes[0:6, L_DOWN + D * q : L_DOWN + D * q + D] = w_down[6 * q : 6 * q + 6, :]
+    lanes[0:6, L_EMBED : L_EMBED + DE] = w_embed[...]
+    s["up16"][...] = jnp.zeros_like(s["up16"])
+    s["up16"][0:6, :] = w_up[...]
+    lane = iota((D, 128), 1)
+    row = iota((D, 128), 0)
+    for n in range(6):
+        col = lane + 128 * n
+        device = (col * 10923) >> 16
+        start = min(24 * (128 * n // 6) // 128 * 128, FF - D)
+        target = 24 * device + (col - 6 * device) - start
+        for q in range(4):
+            part = dot(s["up16"][:, start : start + D], hot(row == target + 6 * q))
+            at = L_UP + D * q + 128 * n
+            lanes[:, at : at + 128] = part.astype(BF)
+    row, col = iota((32, 16), 0), iota((32, 16), 1)
+    for i in range(4):
+        packed = jnp.zeros((32, 512), F32)
+        for k in range(5):
+            first = 2048 * k + 512 * i
+            pick = hot((row == col + 6 * k) & (col < 6))
+            packed = packed + dot(pick, lanes[:, first : first + 512])
+        s["shard"][:, 512 * i : 512 * i + 512] = packed.astype(BF)
+    shard = s["shard"]
     rb, meta_all = s["rb"], s["meta_all"]
+    pl.semaphore_wait(pltpu.get_barrier_semaphore(), callers)
+    meta_sent = []
+    for t in range(1, PLANE):
+        meta_sent.append(links.send(meta, meta_all.at[t], place.plane(t)))
     sent = []
     for t in range(1, PLANE):
         to = place.plane(t)
-        sent.append(links.send(shard.at[to[1]], rb.at[place.fs], to))
-    meta_sent = []
-    for t in range(1, PLANE):
-        meta_sent.append(links.send(meta, meta_all.at[place.fs], place.plane(t)))
-    rb[place.fs] = shard[place.fs]
-    meta_all[place.fs] = meta[...]
+        sent.append(links.send(shard.at[:, cols(to[1], 128)], rb.at[place.fs], to))
+    rb[place.fs] = shard[:, cols(place.fs, 128)]
+    meta_all[0] = meta[...]
     for t in range(1, PLANE):
         source = place.plane(PLANE - t)
         links.arrive(rb.at[source[1]], sent[t - 1], source)
@@ -445,8 +498,7 @@
     later.three()
 
     for t in range(1, PLANE):
-        source = place.plane(PLANE - t)
-        links.arrive(meta_all.at[source[1]], meta_sent[t - 1], source)
+        links.arrive(meta_all.at[t], meta_sent[t - 1], place.plane(PLANE - t))
     cot_load.wait()
 
     def lens_of(m, blk):
@@ -457,12 +509,8 @@
         return lens, starts
 
     total = jnp.zeros((1, DE), F32)
-    orders = [meta[5:6, k : k + 1] for k in range(STRIPS)]
     for k in range(STRIPS):
-        m = jnp.zeros((8, 128), I32)
-        for source in range(PLANE):
-            here = orders[k] == (place.fs + PLANE - source) % PLANE
-            m = jnp.where(here, meta_all[source], m)
+        m = meta_all[route[0, k]]
         blk, j = k // 4, k % 4
         lens, starts = lens_of(m, blk)
         skip = jnp.concatenate([m[2 * blk : 2 * blk + 1], m[2 * blk + 1 : 2 * blk + 2]], 1)
@@ -476,9 +524,9 @@
         lane = iota((WINDOW, SEG), 1).astype(F32)
         spot = iota((WINDOW, SEG), 0).astype(F32)
         perm = hot((spot == lane + through + float(off)) & (lane < lens[j]))
-        s["perm"][k] = perm
+        perms[k] = perm
         picked = tdot(perm, s["dec"][base : base + WINDOW])
-        s["act"][SEG * j : SEG * j + SEG, DE * blk : DE * blk + DE] = picked.astype(BF)
+        s["strip"][k] = picked.astype(BF)
         total = total - col_sum(picked)
 
     def sum_rows(i, acc):
@@ -490,32 +538,27 @@
     s["vgrad"][...] = jnp.zeros_like(s["vgrad"])
     s["vgrad"][V_MASK : V_MASK + 1, 0:DE] = total
 
-    def weight_of(k, value):
-        return jnp.where(orders[k] == value, 1.0, 0.0).astype(BF)
-
-    def fill_slot(t, _):
-        total = jnp.zeros((SEG, DE), BF)
-        for k in range(STRIPS):
-            blk, j = k // 4, k % 4
-            one = s["act"][SEG * j : SEG * j + SEG, DE * blk : DE * blk + DE]
-            total = total + one * weight_of(k, (PLANE - t) % PLANE)
-        s["out_slots"][t] = total
-        return 0
-
-    lax.fori_loop(0, PLANE, fill_slot, 0)
+    s["strip"][STRIPS] = jnp.zeros((SEG, DE), BF)
+    for t in range(PLANE):
+        s["slots"][t] = s["strip"][route[1, (PLANE - t) % PLANE]]
+    slot_store = pltpu.make_async_copy(s["slots"], cot_from, local_sem.at[0])
+    slot_store.start()
+    own_store = pltpu.make_async_copy(s["slots"].at[0], cot_to.at[0], local_sem.at[1])
+    own_store.start()
+
+    slot_store.wait()
+    own_store.wait()
+    cot_sent, cot_copies = [], []
+
+    def send_cot(begin, end):
+        for t in range(begin, end):
+            slot = cot_to.at[PLANE - t]
+            cot_sent.append(links.send(cot_from.at[t], slot, place.plane(t)))
+            cot_copies.append(links.started.pop())
 
     first.four()
-    later.four()
     first.five()
     first.six()
-    later.five()
-    later.six()
-    cot_sent = []
-    for t in range(1, PLANE):
-        cot_sent.append(
-            links.send(s["out_slots"].at[t], s["in_slots"].at[t], place.plane(t))
-        )
-    s["in_slots"][0] = s["out_slots"][0]
 
     chunk = g[0, 0, :, :, :, 0:128].reshape(D, 128)
     table = s["acc"]
@@ -563,7 +606,11 @@
             s["qkv"][rows, cols(t)] = out.astype(BF)
         return 0
 
-    lax.fori_loop(0, 9, qkv_tile, 0)
+    later.four()
+    lax.fori_loop(0, 4, qkv_tile, 0)
+    later.five()
+    send_cot(1, PLANE)
+    lax.fori_loop(4, 9, qkv_tile, 0)
 
     lens_own = [lens_of(meta[...], b) for b in range(2)]
 
@@ -597,6 +644,9 @@
             return 0
 
         lax.fori_loop(0, 6, heads, 0)
+    later.six()
+    links.drain()
+    links.started = cot_copies
 
     def out_tile(t, _):
         out = dot(s["ctx"][...], weight(H_OUT + t)) + vec[6:7, cols(t)]
@@ -635,39 +685,44 @@
         out = dot(s["hb"][...], weight(H_EMBED + t)) + vec[V_BE : V_BE + 1, cols(t)]
         s["emb"][:, cols(t)] = out.astype(BF)
 
-    slot = iota((1, PLANE), 1)
-    slot_start, slot_len = jnp.zeros((1, PLANE), F32), jnp.zeros((1, PLANE), F32)
-    for k in range(STRIPS):
-        blk, j = k // 4, k % 4
+    def strip_hot(blk):
         lens, starts = lens_own[blk]
-        slot_start = jnp.where(orders[k] == slot, starts[j] + 256.0 * blk, slot_start)
-        slot_len = jnp.where(orders[k] == slot, lens[j], slot_len)
-
-    def slot_hot(t):
-        i, r = iota((SEG, ROWS), 0).astype(F32), iota((SEG, ROWS), 1).astype(F32)
-        start, size = slot_start[:, t : t + 1], slot_len[:, t : t + 1]
-        return hot((r - start == i) & (i < size))
+        picks = []
+        for j in range(4):
+            r, t = iota((256, SEG), 0).astype(F32), iota((256, SEG), 1).astype(F32)
+            picks.append(hot((r - starts[j] == t) & (t < lens[j])))
+        return jnp.concatenate(picks, 1)
+
+    for blk in range(2):
+        moved = tdot(strip_hot(blk), s["emb"][256 * blk : 256 * blk + 256])
+        for j in range(4):
+            s["strip"][4 * blk + j] = moved[SEG * j : SEG * j + SEG].astype(BF)
+    for t in range(PLANE):
+        s["slots"][t] = s["strip"][route[1, t]]
+    slot_store = pltpu.make_async_copy(s["slots"], emb_from, local_sem.at[0])
+    slot_store.start()
+    own_store = pltpu.make_async_copy(s["slots"].at[0], emb_to.at[0], local_sem.at[1])
+    own_store.start()
+    slot_store.wait()
+    own_store.wait()
+    emb_sent = []
+
+    def send_emb(first, last):
+        for t in range(first, last):
+            emb_sent.append(links.send(emb_from.at[t], emb_to.at[t], place.plane(t)))
+
+    send_emb(1, PLANE)
 
     for t in range(1, PLANE):
-        links.arrive(s["in_slots"].at[t], cot_sent[t - 1], place.plane(PLANE - t))
+        links.arrive(cot_to.at[PLANE - t], cot_sent[t - 1], place.plane(PLANE - t))
     de = s["emb"]
-    total = jnp.zeros((ROWS, DE), F32)
-    links.drain()
-    for t in range(PLANE):
-        pick = slot_hot(t)
-        total = total + tdot(pick, s["in_slots"][(PLANE - t) % PLANE])
-        s["out_slots"][t] = dot(pick, s["emb"][...]).astype(BF)
-    de[...] = total.astype(BF)
-    for t in range(1, PLANE):
-        pl.semaphore_signal(slot_free, inc=1, device_id=place.plane(t), device_id_type=MESH)
-    pl.semaphore_wait(slot_free, PLANE - 1)
-    emb_sent = []
-    for t in range(1, PLANE):
-        emb_sent.append(
-            links.send(s["out_slots"].at[t], s["in_slots"].at[t], place.plane(t))
-        )
-    s["in_slots"][0] = s["out_slots"][0]
-
+    cot_back = pltpu.make_async_copy(cot_to, s["slots"], local_sem.at[0])
+    cot_back.start()
+    cot_back.wait()
+    for blk in range(2):
+        got = [s["slots"][route[0, 4 * blk + j]] for j in range(4)]
+        moved = dot(strip_hot(blk), jnp.concatenate(got, 0))
+        de[256 * blk : 256 * blk + 256] = moved.astype(BF)
     vg = s["vgrad"]
     vg[V_BE : V_BE + 1, 0:DE] = col_sum(de[...].astype(F32))
     wide = s["wide"]
@@ -731,8 +786,9 @@
     zero = jnp.zeros((1, D), F32)
     vg[2:3], vg[3:4], vg[6:7] = lax.fori_loop(0, 4, norm_two_back, (zero, zero, zero))
 
-    gathers = [Gather(place, links, g, ks, bufs) for ks in GROUPS]
-    g_first, g_later = gathers
+    g_first, g_mid, g_later = [Gather(place, links, g, ks, bufs) for ks in SUM_GROUPS]
+    g_mid.core_first = 1
+    g_later.one()
 
     def out_back(i, _):
         rows = cols(i)
@@ -771,7 +827,13 @@
             s["qkv"][rows, cols(12 + hp, 128)] = jnp.where(lo, dv[0], dv[1]).astype(BF)
             return 0
 
-        lax.fori_loop(0, 6, heads_back, 0)
+        lax.fori_loop(0, 6, heads_back, 0, unroll=2)
+        if blk == 0:
+            g_later.two()
+            sibling = place.sibling()
+            pl.semaphore_signal(core_free, inc=1, device_id=sibling, device_id_type=MESH)
+        else:
+            g_later.three()
 
     def bias_sums(i, sums):
         rows = cols(i, 64)
@@ -787,7 +849,7 @@
             total = dot_t(s["qkv"][rows, cols(3 * q)], weight(H_QKV + 3 * q))
             for t in range(1, 3):
                 total = total + dot_t(s["qkv"][rows, cols(3 * q + t)], weight(H_QKV + 3 * q + t))
-            acc[rows, :] = jnp.where(q == 0, total, acc[rows, :] + total)
+            acc[rows, :] = jnp.where(q == 2, total, acc[rows, :] + total)
             return 0
 
         lax.fori_loop(0, 2, rows_part, 0)
@@ -795,7 +857,12 @@
             put_grad(H_QKV + 3 * q + t, tdot(s["n1"][...], s["qkv"][:, cols(3 * q + t)]))
         return 0
 
-    lax.fori_loop(0, 3, qkv_part, 0)
+    qkv_part(2, 0)
+    pl.semaphore_wait(core_free, 1)
+    g_mid.one()
+    g_later.four()
+    lax.fori_loop(0, 2, qkv_part, 0)
+    g_mid.two()
 
     def norm_one_back(i, sums):
         rows = cols(i, 128)
@@ -833,43 +900,18 @@
     chunk = lax.fori_loop(0, 2, fold_four, chunk)
     g[0, 0, :, :, :, 0:128] = chunk.astype(BF).reshape(4, 2, 96, 128)
 
-    g_later.one()
-    g_later.two()
-    pl.semaphore_signal(core_free, inc=1, device_id=place.sibling(), device_id_type=MESH)
-    pl.semaphore_wait(core_free, 1)
     g_first.one()
+    vec_out[...] = vec[V_MASK : V_MASK + 1, :]
+    g_later.five()
+    g_mid.three()
     g_first.two()
-    for t in range(1, PLANE):
-        links.arrive(s["in_slots"].at[t], emb_sent[t - 1], place.plane(PLANE - t))
-    mask = vec[V_MASK : V_MASK + 1, 0:DE]
-    blank = jnp.broadcast_to(mask.astype(BF), (16, DE))
-
-    def fill(i, _):
-        s["dec"][cols(i, 16), :] = blank
-        return 0
-
-    lax.fori_loop(0, OUT_ROWS // 16, fill, 0)
-    s["dec"][OUT_ROWS - 8 :, :] = blank[0:8]
-    for k in range(STRIPS):
-        perm = s["perm"][k]
-        base = STRIP_POS * k - (STRIP_POS * k) % 16
-
-        def find(t, total):
-            return total + s["in_slots"][t] * weight_of(k, t)
-
-        strip = lax.fori_loop(0, PLANE, find, jnp.zeros((SEG, DE), BF))
-        placed = dot(perm, strip)
-        filled = jnp.sum(perm.astype(F32), -1, keepdims=True)
-        s["dec"][base : base + WINDOW] = jnp.where(filled > 0.5, placed, mask).astype(BF)
-    dec_store = pltpu.make_async_copy(s["dec"], dec_out, local_sem.at[0])
-    dec_store.start()
-    g_later.three()
+    g_later.six()
+    g_mid.four()
     g_first.three()
-    g_later.four()
+    g_mid.five()
     g_first.four()
-    g_later.five()
+    g_mid.six()
     g_first.five()
-    g_later.six()
     g_first.six()
     row, col = iota((PLANE * 32, 96), 0), iota((PLANE * 32, 96), 1)
     inner_row = row & 31
@@ -883,76 +925,155 @@
     fin_sent = []
     for t in range(1, PLANE):
         to = place.plane(t)
-        fin_sent.append(links.send(s["fin_send"].at[to[1]], s["fin_recv"].at[place.fs], to))
-    s["fin_recv"][place.fs] = s["fin_send"][place.fs]
+        slot = s["fin_recv"].at[:, cols(place.fs, 128)]
+        fin_sent.append(links.send(s["fin_send"].at[to[1]], slot, to))
+    s["fin_recv"][:, cols(place.fs, 128)] = s["fin_send"][place.fs]
     for t in range(1, PLANE):
         source = place.plane(PLANE - t)
-        links.arrive(s["fin_recv"].at[source[1]], fin_sent[t - 1], source)
+        links.arrive(s["fin_recv"].at[:, cols(source[1], 128)], fin_sent[t - 1], source)
     fin[...] = s["fin_recv"][...]
+    for t in range(1, PLANE):
+        links.arrive(emb_to.at[t], emb_sent[t - 1], place.plane(PLANE - t))
     links.drain()
-    dec_store.wait()
     patch_store.wait()
 
 
-def mega(shard, meta, x, cot):
+def mega(w_qkv, w_out, w_up, w_down, w_embed, vectors, skipped, lengths, route, x, cot):
     dma = pltpu.SemaphoreType.DMA
     vmem = pl.BlockSpec(memory_space=pltpu.VMEM)
+    smem = pl.BlockSpec(memory_space=pltpu.SMEM)
     hbm = pl.BlockSpec(memory_space=pl.ANY)
     return pl.pallas_call(
         kernel,
         out_shape=(
-            jax.ShapeDtypeStruct((OUT_ROWS, DE), BF),
             jax.ShapeDtypeStruct((ROWS, D), F32),
-            jax.ShapeDtypeStruct((PLANE, 32, 128), BF),
-        ),
-        in_specs=[vmem, vmem, vmem, hbm],
-        out_specs=(hbm, hbm, vmem),
+            jax.ShapeDtypeStruct((32, 2048), BF),
+            jax.ShapeDtypeStruct((STRIPS, WINDOW, SEG), BF),
+            jax.ShapeDtypeStruct((1, D), F32),
+        )
+        + (jax.ShapeDtypeStruct((PLANE, SEG, DE), BF),) * 4,
+        in_specs=[vmem] * 8 + [smem, vmem, hbm],
+        out_specs=(hbm, vmem, vmem, vmem) + (hbm,) * 4,
         scratch_shapes=[pltpu.VMEM(shape, kind) for shape, kind in SCRATCH.values()]
         + [pltpu.VMEM(shape, BF) for shape in reduce_bufs()]
-        + [dma((N_SEM,)), dma((N_SEM,)), dma((2,)), pltpu.SemaphoreType.REGULAR, pltpu.SemaphoreType.REGULAR],
+        + [dma((N_SEM,)), dma((N_SEM,)), dma((2,))]
+        + [pltpu.SemaphoreType.REGULAR],
         compiler_params=pltpu.CompilerParams(
             collective_id=1, has_side_effects=True, vmem_limit_bytes=64 * 1024 * 1024
         ),
         name="layer",
-    )(shard, meta, x, cot)
+    )(w_qkv, w_out, w_up, w_down, w_embed, vectors, skipped, lengths, route, x, cot)
+
+
+VECTOR_AT = (0, 6, 12, 18, 24, 30, 36, 48, 42, 72, 76)
+VECTOR_SIZE = (6, 6, 6, 6, 6, 6, 6, 24, 6, 4, 4)
+
+
+def finish_kernel(route, patch, fin, perms, mask, emb, dec_out, patch_out, g_qkv, g_out, g_up,
+                  g_down, g_embed, *rest):
+    vectors, (dec, wide, strips, rows, sems) = rest[:11], rest[11:]
+    loads = []
+    for k in range(STRIPS):
+        source = emb.at[route[0, k]]
+        loads.append(pltpu.make_async_copy(source, strips.at[k], sems.at[2 + k]))
+        loads[-1].start()
+    patch_load = pltpu.make_async_copy(patch, rows, sems.at[0])
+    patch_load.start()
+    token = mask[0:1, 0:DE]
+    blank = jnp.broadcast_to(token.astype(BF), (64, DE))
+
+    def fill(i, _):
+        dec[pl.ds(pl.multiple_of(i * 64, 64), 64), :] = blank
+        return 0
+
+    lax.fori_loop(0, OUT_ROWS // 64, fill, 0)
+    dec[OUT_ROWS - 8 :, :] = blank[0:8]
+    for k in range(STRIPS):
+        perm = perms[k]
+        base = STRIP_POS * k - (STRIP_POS * k) % 16
+        filled = dot(perm, jnp.ones((SEG, 128), BF))[:, 0:1]
+        loads[k].wait()
+        placed = dot(perm, strips[k])
+        dec[base : base + WINDOW] = jnp.where(filled > 0.5, placed, token).astype(BF)
+    dec_store = pltpu.make_async_copy(dec, dec_out, sems.at[1])
+    dec_store.start()
+    patch_load.wait()
+    patch_store = pltpu.make_async_copy(rows, patch_out, sems.at[0])
+    patch_store.start()
+    row, col = iota((8, 32), 0), iota((8, 32), 1)
+    for k in range(5):
+        pick = hot((col == row + 6 * k) & (row < 6))
+        wide[:, 2048 * k : 2048 * k + 2048] = dot(pick, fin[...])
+    g_qkv[...] = wide[0:6, L_QKV:L_OUT]
+    g_out[...] = wide[0:6, L_OUT:L_UP]
+    for q in range(4):
+        g_down[6 * q : 6 * q + 6, :] = wide[0:6, L_DOWN + D * q : L_DOWN + D * q + D]
+    g_embed[...] = wide[0:6, L_EMBED : L_EMBED + DE]
+    col = iota((256, 384), 1)
+    device = (col * 2731) >> 16
+    inner = col - 24 * device
+    part = (inner * 43) >> 8
+    source = 6 * device + (inner - 6 * part)
+    row = iota((256, 384), 0)
+    for shift in range(4):
+        pick = [hot((part == q) & (row == source + (96 * shift) % 128)) for q in range(4)]
+        for m in (shift, shift + 4):
+            start = L_UP + (96 * m) // 128 * 128
+            total = jnp.zeros((8, 384), F32)
+            for q in range(4):
+                window = wide[:, start + D * q : start + D * q + 256].astype(BF)
+                total = total + dot(window, pick[q])
+            g_up[:, 384 * m : 384 * m + 384] = total[0:6]
+    for ref, at, size in zip(vectors, VECTOR_AT, VECTOR_SIZE):
+        ref[...] = wide[0, at : at + size]
+    patch_store.wait()
+    dec_store.wait()
+
+
+def finish(route, patch, fin, perms, mask, emb):
+    vmem = pl.BlockSpec(memory_space=pltpu.VMEM)
+    hbm = pl.BlockSpec(memory_space=pl.ANY)
+    shape = jax.ShapeDtypeStruct
+    return pl.pallas_call(
+        finish_kernel,
+        out_shape=(shape((OUT_ROWS, DE), BF), shape((ROWS, D), F32))
+        + tuple(shape(s, F32) for s in ((6, 3 * D), (6, D), (6, FF), (24, D), (6, DE)))
+        + tuple(shape((n,), F32) for n in VECTOR_SIZE),
+        in_specs=[pl.BlockSpec(memory_space=pltpu.SMEM), hbm, vmem, vmem, vmem, hbm],
+        out_specs=(hbm, hbm) + (vmem,) * 16,
+        scratch_shapes=[
+            pltpu.VMEM((OUT_ROWS, DE), BF),
+            pltpu.VMEM((8, 10240), F32),
+            pltpu.VMEM((STRIPS, SEG, DE), BF),
+            pltpu.VMEM((ROWS, D), F32),
+            pltpu.SemaphoreType.DMA((2 + STRIPS,)),
+        ],
+        compiler_params=pltpu.CompilerParams(vmem_limit_bytes=64 * 1024 * 1024),
+        name="finish",
+    )(route, patch, fin, perms, mask, emb)
 
 
 def on_device(patches, lengths, skipped, strip_order, decoder_grad, qkv_weight, out_weight,
               up_weight, down_weight, embed_weight, gain_one, shift_one, gain_two, shift_two,
               bias_query, bias_value, bias_out, bias_up, bias_down, bias_embed, mask_token):
-    vectors = jnp.concatenate(
-        [gain_one, shift_one, gain_two, shift_two, bias_query, bias_value, bias_out, bias_down,
-         bias_up, bias_embed, mask_token]
+    pieces = (gain_one, shift_one, gain_two, shift_two, bias_query, bias_value, bias_out,
+              bias_down, bias_up, bias_embed, mask_token)
+    vectors, at = None, 0
+    for piece in pieces:
+        size = piece.shape[0]
+        padded = jnp.pad(piece, (at, 128 - at - size))
+        vectors = padded if vectors is None else vectors + padded
+        at += size
+    strip = lax.broadcasted_iota(I32, (PLANE, STRIPS), 1)
+    place = lax.broadcasted_iota(I32, (PLANE, STRIPS), 0)
+    match = (strip_order[0, None, 0:STRIPS] == place).astype(I32)
+    inverse = STRIPS + jnp.sum(match * (strip - STRIPS), 1)
+    route = jnp.stack([strip_order[0], inverse])
+    patch_grad, fin, perms, mask, _, _, _, emb = mega(
+        qkv_weight, out_weight, up_weight, down_weight, embed_weight, vectors[None],
+        skipped.reshape(4, 128), lengths, route, patches, decoder_grad,
     )
-    up = up_weight.reshape(6, 128, 4, 6).transpose(0, 2, 1, 3).reshape(6, FF)
-    down = down_weight.reshape(4, 6, D).transpose(1, 0, 2).reshape(6, FF)
-    first = jnp.zeros((6, 256), BF).at[0, 0:80].set(vectors)
-    last = jnp.zeros((6, 256), BF)
-    lanes = jnp.concatenate([first, qkv_weight, out_weight, up, down, embed_weight, last], 1)
-    shard = lanes.reshape(6, 5, PLANE, 128).transpose(2, 1, 0, 3).reshape(PLANE, 30, 128)
-    shard = jnp.pad(shard, ((0, 0), (0, 2), (0, 0)))
-    meta = jnp.concatenate(
-        [
-            skipped.reshape(4, 128),
-            jnp.pad(lengths.reshape(1, 8), ((0, 0), (0, 120))),
-            jnp.pad(strip_order, ((0, 2), (0, 112))),
-        ],
-        0,
-    )
-    dec, patch_grad, fin = mega(shard, meta, patches, decoder_grad)
-    fin = fin[:, 0:30].reshape(PLANE, 5, 6, 128).transpose(2, 1, 0, 3).reshape(6, 10240)
-    fin = fin.astype(F32)
-    parts = []
-    at = 256
-    for width in (3 * D, D, FF, FF, DE):
-        parts.append(fin[:, at : at + width])
-        at += width
-    g_qkv, g_out, g_up, g_down, g_embed = parts
-    g_up = g_up.reshape(6, 4, 128, 6).transpose(0, 2, 1, 3).reshape(6, FF)
-    g_down = g_down.reshape(6, 4, D).transpose(1, 0, 2).reshape(24, D)
-    v = fin[0, 0:80]
-    return (dec, patch_grad, g_qkv, g_out, g_up, g_down, g_embed, v[0:6], v[6:12], v[12:18],
-            v[18:24], v[24:30], v[30:36], v[36:42], v[48:72], v[42:48], v[72:76], v[76:80])
+    return tuple(finish(route, patch_grad, fin, perms, mask, emb))
 
 
 def solution(mesh):

time: 237 us -> 188 us (0.79)
  local copies, waits for them, and re-layouts: 30 us -> 0.66 us
  Pallas kernels: 204 us -> 183 us
    pallas_call x1 -> x2, Pallas kernels: 204 us -> 183 us  [the longest x1 175 us: mega(): pl.pallas_call(kernel, out_shape=(jax.ShapeDtypeStruct((ROWS, D), F32), j...]
    reshape x8 -> x0, local copies, waits for them, and re-layouts: 9.49 us -> none  [the longest x2 3.64 us: on_device(): g_up = g_up.reshape(6, 4, 128, 6).transpose(0, 2, 1, 3).reshape(6, FF)]
    concatenate x2 -> x0, local copies, waits for them, and re-layouts: 7.44 us -> none  [the longest x1 7.43 us: on_device(): jnp.concatenate([gain_one, shift_one, gain_two, shift_two, bias_query, bi...]
    unnamed x13 -> x0, local copies, waits for them, and re-layouts: 7.42 us -> none
    slice x7 -> x0, local copies, waits for them, and re-layouts: 3.64 us -> none  [the longest x4 1.87 us: on_device(): parts.append(fin[:, at:at + width])]
where the time goes in v2:
time: 188 us; the launch traced here: 187 us
  Pallas kernels  183 us (97%)
  other arithmetic  2.68 us (1%)
    pallas_call x1, Pallas kernels, mega(): pl.pallas_call(kernel, out_shape=(jax.ShapeDtypeStruct((ROWS, D), F32), j...  175 us
    pallas_call x1, Pallas kernels, finish(): pl.pallas_call(finish_kernel, out_shape=(shape((OUT_ROWS, DE), BF), shape...  7.65 us

profile of v2, /device:TPU:0, one launch (start us, length us, event | category | flops | bytes accessed | tf_op | source)
XLA Modules:
  0.0 187.3 jit_solution(9440757990647815091)
XLA Ops:
  0.7 1.4 add_bitcast_fusion.vectors
  2.1 0.7 slice_bitcast_fusion
  2.7 0.1 select_reduce_fusion
  2.8 1.2 pad_add_fusion.route
  4.0 175.5 %layer.1 = (f32[512,768]{1,0:T(8,128)}, bf16[32,2048]{1,0:T(8,128)(2,1)}, bf16[8,272,128]{2,1,0:T(8,128)(2,1)}, f32[1,768]{1,0:T(1,128)}, bf16[16,128,512]{2,1,0...) custom-call(bf16[6,2304]{1,0:T(8,128)(2,1)} %w_qkv.1, ...), custom_call_target="tpu_custom_call" | custom-call | tf_op jit(solution)/shard_map/layer/pallas_call | solution.py:946
  179.5 7.7 %finish.1 = (bf16[4232,512]{1,0:T(8,128)(2,1)}, f32[512,768]{1,0:T(8,128)}, f32[6,2304]{1,0:T(8,128)}, f32[6,768]{1,0:T(8,128)}, f32[6,3072]{1,0:T(8,128)}, /*in...) custom-call(s32[2,16]{1,0:T(2,128)} %pad_add_fusion.route, ...), custom_call_target="tpu_custom_call" | custom-call | tf_op jit(solution)/shard_map/finish/pallas_call | solution.py:1037
  (2 shorter events, 0.0 us)

commit v3 on v2

--- a/solution.py
+++ b/solution.py
@@ -240,6 +240,9 @@
             for y in range(4) if coords["y"] is None else (coords["y"],):
                 for z in range(4) if coords["z"] is None else (coords["z"],):
                     place = (k, y, z, self.p.c, pl.ds(start, count), xs)
+                    if len(reads) == 1:
+                        self.g[place] = self.g[place] + reads[0](k, y, z)
+                        continue
                     total = self.g[place].astype(F32)
                     for read in reads:
                         total = total + read(k, y, z).astype(F32)
@@ -399,6 +402,7 @@
     "dec": ((OUT_ROWS, DE), BF),
     "slots": ((PLANE, SEG, DE), BF),
 }
+FLIPPED = {"hb": 0, "ctx": D, "act": 2 * D, "n1": 2560, "n2": 2560 + D}
 N_SEM = 260
 
 
@@ -557,8 +561,14 @@
             cot_copies.append(links.started.pop())
 
     first.four()
+    later.four()
     first.five()
+    later.five()
     first.six()
+    later.six()
+    links.drain()
+    send_cot(1, PLANE)
+    links.started = cot_copies
 
     chunk = g[0, 0, :, :, :, 0:128].reshape(D, 128)
     table = s["acc"]
@@ -597,7 +607,7 @@
         s["n1"][rows, :] = (hat * vec[0:1] + vec[1:2]).astype(BF)
         return 0
 
-    lax.fori_loop(0, 4, norm_one, 0)
+    lax.fori_loop(0, 4, norm_one, 0, unroll=2)
 
     def qkv_tile(t, _):
         for i in range(2):
@@ -606,11 +616,7 @@
             s["qkv"][rows, cols(t)] = out.astype(BF)
         return 0
 
-    later.four()
-    lax.fori_loop(0, 4, qkv_tile, 0)
-    later.five()
-    send_cot(1, PLANE)
-    lax.fori_loop(4, 9, qkv_tile, 0)
+    lax.fori_loop(0, 9, qkv_tile, 0, unroll=3)
 
     lens_own = [lens_of(meta[...], b) for b in range(2)]
 
@@ -643,17 +649,14 @@
             s["ctx"][rows, cols(hp, 128)] = jnp.where(lane < 64, outs[0], outs[1]).astype(BF)
             return 0
 
-        lax.fori_loop(0, 6, heads, 0)
-    later.six()
-    links.drain()
-    links.started = cot_copies
+        lax.fori_loop(0, 6, heads, 0, unroll=2)
 
     def out_tile(t, _):
         out = dot(s["ctx"][...], weight(H_OUT + t)) + vec[6:7, cols(t)]
         s["h1"][:, cols(t)] = x_ref[:, cols(t)].astype(F32) + out
         return 0
 
-    lax.fori_loop(0, 3, out_tile, 0)
+    lax.fori_loop(0, 3, out_tile, 0, unroll=3)
 
     def norm_two(i, _):
         rows = cols(i, 128)
@@ -661,7 +664,7 @@
         s["n2"][rows, :] = (hat * vec[2:3] + vec[3:4]).astype(BF)
         return 0
 
-    lax.fori_loop(0, 4, norm_two, 0)
+    lax.fori_loop(0, 4, norm_two, 0, unroll=2)
 
     def up_tile(t, _):
         for i in range(2):
@@ -673,7 +676,7 @@
             s["slope"][rows, cols(t)] = (phi + u * density).astype(BF)
         return 0
 
-    lax.fori_loop(0, 12, up_tile, 0)
+    lax.fori_loop(0, 12, up_tile, 0, unroll=2)
     for t in range(3):
         for i in range(2):
             rows = cols(i)
@@ -713,6 +716,18 @@
 
     send_emb(1, PLANE)
 
+    def flipped(name):
+        return s["dec"][FLIPPED[name] : FLIPPED[name] + D, :]
+
+    for name in ("n1", "n2", "ctx", "hb"):
+
+        def flip(i, _, name=name):
+            at = pl.ds(pl.multiple_of(FLIPPED[name] + 128 * i, 128), 128)
+            s["dec"][at, :] = s[name][:, cols(i, 128)].T
+            return 0
+
+        lax.fori_loop(0, 6, flip, 0)
+
     for t in range(1, PLANE):
         links.arrive(cot_to.at[PLANE - t], cot_sent[t - 1], place.plane(PLANE - t))
     de = s["emb"]
@@ -734,9 +749,9 @@
         s["low"][rows, :] = dh.astype(BF)
         return acc + col_sum(dh)
 
-    vg[7:8] = lax.fori_loop(0, 2, embed_back, jnp.zeros((1, D), F32))
+    vg[7:8] = lax.fori_loop(0, 2, embed_back, jnp.zeros((1, D), F32), unroll=2)
     for t in range(2):
-        put_grad(H_EMBED + t, tdot(s["hb"][...], de[:, cols(t)]))
+        put_grad(H_EMBED + t, dot(flipped("hb"), de[:, cols(t)]))
 
     def down_part(q, _):
 
@@ -749,10 +764,12 @@
             s["slope"][rows, cols(q, D)] = du
             return acc + col_sum(du.astype(F32))
 
-        vg[pl.ds(8 + q, 1), :] = lax.fori_loop(0, 2, rows_part, jnp.zeros((1, D), F32))
-        a = s["act"][:, cols(q, D)]
+        vg[pl.ds(8 + q, 1), :] = lax.fori_loop(0, 2, rows_part, jnp.zeros((1, D), F32), unroll=2)
+        for i in range(6):
+            at = FLIPPED["act"] + 128 * i
+            s["dec"][at : at + 128, :] = s["act"][:, cols(6 * q + i, 128)].T
         for t in range(3):
-            put_grad(H_DOWN + 3 * q + t, tdot(a, s["low"][:, cols(t)]))
+            put_grad(H_DOWN + 3 * q + t, dot(flipped("act"), s["low"][:, cols(t)]))
         return 0
 
     lax.fori_loop(0, 4, down_part, 0)
@@ -767,9 +784,9 @@
             acc[rows, :] = jnp.where(q == 0, total, acc[rows, :] + total)
             return 0
 
-        lax.fori_loop(0, 2, rows_part, 0)
+        lax.fori_loop(0, 2, rows_part, 0, unroll=2)
         for t in range(3):
-            put_grad(H_UP + 3 * q + t, tdot(s["n2"][...], s["slope"][:, cols(3 * q + t)]))
+            put_grad(H_UP + 3 * q + t, dot(flipped("n2"), s["slope"][:, cols(3 * q + t)]))
         return 0
 
     lax.fori_loop(0, 4, up_part, 0)
@@ -784,7 +801,7 @@
         return (sums[0] + col_sum(dn * hat), sums[1] + col_sum(dn), sums[2] + col_sum(dh))
 
     zero = jnp.zeros((1, D), F32)
-    vg[2:3], vg[3:4], vg[6:7] = lax.fori_loop(0, 4, norm_two_back, (zero, zero, zero))
+    vg[2:3], vg[3:4], vg[6:7] = lax.fori_loop(0, 4, norm_two_back, (zero, zero, zero), unroll=2)
 
     g_first, g_mid, g_later = [Gather(place, links, g, ks, bufs) for ks in SUM_GROUPS]
     g_mid.core_first = 1
@@ -798,12 +815,16 @@
         s["hb"][rows, :] = total.astype(BF)
         return 0
 
-    lax.fori_loop(0, 2, out_back, 0)
+    lax.fori_loop(0, 2, out_back, 0, unroll=2)
     for t in range(3):
-        put_grad(H_OUT + t, tdot(s["ctx"][...], s["low"][:, cols(t)]))
+        put_grad(H_OUT + t, dot(flipped("ctx"), s["low"][:, cols(t)]))
 
     for blk in range(2):
         rows = slice(256 * blk, 256 * blk + 256)
+
+        def put(chunk, value, blk=blk):
+            at = pl.ds(pl.multiple_of(512 * (chunk // 4) + 256 * blk, 256), 256)
+            s["dec"][at, cols(chunk % 4, 128)] = value.astype(BF)
 
         def heads_back(hp, _):
             q2 = s["qkv"][rows, cols(hp, 128)]
@@ -822,9 +843,9 @@
                 dk.append(tdot(ds, q2))
                 dv.append(tdot(p, do2))
             lo = lane < 64
-            s["qkv"][rows, cols(hp, 128)] = (jnp.where(lo, dq[0], dq[1]) * 0.125).astype(BF)
-            s["qkv"][rows, cols(6 + hp, 128)] = (jnp.where(lo, dk[0], dk[1]) * 0.125).astype(BF)
-            s["qkv"][rows, cols(12 + hp, 128)] = jnp.where(lo, dv[0], dv[1]).astype(BF)
+            put(hp, jnp.where(lo, dq[0], dq[1]) * 0.125)
+            put(6 + hp, jnp.where(lo, dk[0], dk[1]) * 0.125)
+            put(12 + hp, jnp.where(lo, dv[0], dv[1]))
             return 0
 
         lax.fori_loop(0, 6, heads_back, 0, unroll=2)
@@ -835,32 +856,35 @@
         else:
             g_later.three()
 
+    def dqkv(t, start=0, size=ROWS):
+        rows = pl.ds(pl.multiple_of(512 * (t // 2) + start, 64), size)
+        return s["dec"][rows, cols(t % 2)]
+
     def bias_sums(i, sums):
-        rows = cols(i, 64)
-        q = s["qkv"][rows, 0:D].astype(F32)
-        v = s["qkv"][rows, 2 * D :].astype(F32)
+        q = [dqkv(t, 64 * i, 64).astype(F32) for t in (0, 1, 2)]
+        v = [dqkv(t, 64 * i, 64).astype(F32) for t in (6, 7, 8)]
+        q, v = [jnp.concatenate(part, 1) for part in (q, v)]
         return (sums[0] + col_sum(q), sums[1] + col_sum(v))
 
-    vg[4:5], vg[5:6] = lax.fori_loop(0, 8, bias_sums, (zero, zero))
+    vg[4:5], vg[5:6] = lax.fori_loop(0, 8, bias_sums, (zero, zero), unroll=2)
 
     def qkv_part(q, _):
         def rows_part(i, _):
             rows = cols(i)
-            total = dot_t(s["qkv"][rows, cols(3 * q)], weight(H_QKV + 3 * q))
+            total = dot_t(dqkv(3 * q, 256 * i, 256), weight(H_QKV + 3 * q))
             for t in range(1, 3):
-                total = total + dot_t(s["qkv"][rows, cols(3 * q + t)], weight(H_QKV + 3 * q + t))
+                total = total + dot_t(dqkv(3 * q + t, 256 * i, 256), weight(H_QKV + 3 * q + t))
             acc[rows, :] = jnp.where(q == 2, total, acc[rows, :] + total)
             return 0
 
-        lax.fori_loop(0, 2, rows_part, 0)
+        lax.fori_loop(0, 2, rows_part, 0, unroll=2)
         for t in range(3):
-            put_grad(H_QKV + 3 * q + t, tdot(s["n1"][...], s["qkv"][:, cols(3 * q + t)]))
+            put_grad(H_QKV + 3 * q + t, dot(flipped("n1"), dqkv(3 * q + t)))
         return 0
 
     qkv_part(2, 0)
     pl.semaphore_wait(core_free, 1)
     g_mid.one()
-    g_later.four()
     lax.fori_loop(0, 2, qkv_part, 0)
     g_mid.two()
 
@@ -871,7 +895,7 @@
         wide[rows, :] = wide[rows, :] + norm_back(dn, vec[0:1], hat, factor)
         return (sums[0] + col_sum(dn * hat), sums[1] + col_sum(dn))
 
-    vg[0:1], vg[1:2] = lax.fori_loop(0, 4, norm_one_back, (zero, zero))
+    vg[0:1], vg[1:2] = lax.fori_loop(0, 4, norm_one_back, (zero, zero), unroll=2)
     patch_store = pltpu.make_async_copy(wide, patch_out, local_sem.at[1])
     patch_store.start()
 
@@ -902,16 +926,17 @@
 
     g_first.one()
     vec_out[...] = vec[V_MASK : V_MASK + 1, :]
+    g_later.four()
+    g_first.two()
+    g_mid.three()
     g_later.five()
-    g_mid.three()
-    g_first.two()
+    g_first.three()
+    g_mid.four()
     g_later.six()
-    g_mid.four()
-    g_first.three()
+    g_first.four()
     g_mid.five()
-    g_first.four()
+    g_first.five()
     g_mid.six()
-    g_first.five()
     g_first.six()
     row, col = iota((PLANE * 32, 96), 0), iota((PLANE * 32, 96), 1)
     inner_row = row & 31

time: 188 us -> 176 us (0.936)
  Pallas kernels: 183 us -> 171 us
    pallas_call x1, Pallas kernels: 175 us -> 163 us  [mega(): pl.pallas_call(kernel, out_shape=(jax.ShapeDtypeStruct((ROWS, D), F32), j...]
where the time goes in v3:
time: 176 us; the launch traced here: 175 us
  Pallas kernels  171 us (97%)
  other arithmetic  2.68 us (2%)
    pallas_call x1, Pallas kernels, mega(): pl.pallas_call(kernel, out_shape=(jax.ShapeDtypeStruct((ROWS, D), F32), j...  163 us
    pallas_call x1, Pallas kernels, finish(): pl.pallas_call(finish_kernel, out_shape=(shape((OUT_ROWS, DE), BF), shape...  7.64 us

profile of v3, /device:TPU:0, one launch (start us, length us, event | category | flops | bytes accessed | tf_op | source)
XLA Modules:
  0.0 175.3 jit_solution(9531727509984130331)
XLA Ops:
  0.7 1.4 add_bitcast_fusion.vectors
  2.1 0.7 slice_bitcast_fusion
  2.7 0.1 select_reduce_fusion
  2.8 1.2 pad_add_fusion.route
  4.0 163.5 %layer.1 = (f32[512,768]{1,0:T(8,128)}, bf16[32,2048]{1,0:T(8,128)(2,1)}, bf16[8,272,128]{2,1,0:T(8,128)(2,1)}, f32[1,768]{1,0:T(1,128)}, bf16[16,128,512]{2,1,0...) custom-call(bf16[6,2304]{1,0:T(8,128)(2,1)} %w_qkv.1, ...), custom_call_target="tpu_custom_call" | custom-call | tf_op jit(solution)/shard_map/layer/pallas_call | solution.py:971
  167.5 7.6 %finish.1 = (bf16[4232,512]{1,0:T(8,128)(2,1)}, f32[512,768]{1,0:T(8,128)}, f32[6,2304]{1,0:T(8,128)}, f32[6,768]{1,0:T(8,128)}, f32[6,3072]{1,0:T(8,128)}, /*in...) custom-call(s32[2,16]{1,0:T(2,128)} %pad_add_fusion.route, ...), custom_call_target="tpu_custom_call" | custom-call | tf_op jit(solution)/shard_map/finish/pallas_call | solution.py:1062
  (2 shorter events, 0.0 us)

commit v4 on v3

--- a/solution.py
+++ b/solution.py
@@ -728,12 +728,17 @@
 
         lax.fori_loop(0, 6, flip, 0)
 
+    cot_back = [pltpu.make_async_copy(cot_to.at[0], s["slots"].at[0], local_sem.at[2])]
+    cot_back[0].start()
     for t in range(1, PLANE):
-        links.arrive(cot_to.at[PLANE - t], cot_sent[t - 1], place.plane(PLANE - t))
+        slot = PLANE - t
+        links.arrive(cot_to.at[slot], cot_sent[t - 1], place.plane(PLANE - t))
+        to = s["slots"].at[slot]
+        cot_back.append(pltpu.make_async_copy(cot_to.at[slot], to, local_sem.at[2 + t]))
+        cot_back[t].start()
     de = s["emb"]
-    cot_back = pltpu.make_async_copy(cot_to, s["slots"], local_sem.at[0])
-    cot_back.start()
-    cot_back.wait()
+    for copy in cot_back:
+        copy.wait()
     for blk in range(2):
         got = [s["slots"][route[0, 4 * blk + j]] for j in range(4)]
         moved = dot(strip_hot(blk), jnp.concatenate(got, 0))
@@ -791,6 +796,10 @@
 
     lax.fori_loop(0, 4, up_part, 0)
 
+    g_first, g_mid, g_later = [Gather(place, links, g, ks, bufs) for ks in SUM_GROUPS]
+    g_mid.core_first = 1
+    g_later.one()
+
     def norm_two_back(i, sums):
         rows = cols(i, 128)
         hat, factor = hat_of(s["h1"][rows, :])
@@ -803,9 +812,6 @@
     zero = jnp.zeros((1, D), F32)
     vg[2:3], vg[3:4], vg[6:7] = lax.fori_loop(0, 4, norm_two_back, (zero, zero, zero), unroll=2)
 
-    g_first, g_mid, g_later = [Gather(place, links, g, ks, bufs) for ks in SUM_GROUPS]
-    g_mid.core_first = 1
-    g_later.one()
 
     def out_back(i, _):
         rows = cols(i)
@@ -981,7 +987,7 @@
         out_specs=(hbm, vmem, vmem, vmem) + (hbm,) * 4,
         scratch_shapes=[pltpu.VMEM(shape, kind) for shape, kind in SCRATCH.values()]
         + [pltpu.VMEM(shape, BF) for shape in reduce_bufs()]
-        + [dma((N_SEM,)), dma((N_SEM,)), dma((2,))]
+        + [dma((N_SEM,)), dma((N_SEM,)), dma((2 + PLANE,))]
         + [pltpu.SemaphoreType.REGULAR],
         compiler_params=pltpu.CompilerParams(
             collective_id=1, has_side_effects=True, vmem_limit_bytes=64 * 1024 * 1024

time: 176 us -> 176 us (level)
  no operation moved by 1% of the time
where the time goes in v4:
time: 176 us
  Pallas kernels  172 us (98%)
  other arithmetic  2.68 us (2%)
    pallas_call x1, Pallas kernels, mega(): pl.pallas_call(kernel, out_shape=(jax.ShapeDtypeStruct((ROWS, D), F32), j...  164 us
    pallas_call x1, Pallas kernels, finish(): pl.pallas_call(finish_kernel, out_shape=(shape((OUT_ROWS, DE), BF), shape...  7.65 us

profile of v4, /device:TPU:0, one launch (start us, length us, event | category | flops | bytes accessed | tf_op | source)
XLA Modules:
  0.0 175.9 jit_solution(12039837413580092073)
XLA Ops:
  0.7 1.4 add_bitcast_fusion.vectors
  2.1 0.7 slice_bitcast_fusion
  2.7 0.1 select_reduce_fusion
  2.8 1.2 pad_add_fusion.route
  4.0 164.1 %layer.1 = (f32[512,768]{1,0:T(8,128)}, bf16[32,2048]{1,0:T(8,128)(2,1)}, bf16[8,272,128]{2,1,0:T(8,128)(2,1)}, f32[1,768]{1,0:T(1,128)}, bf16[16,128,512]{2,1,0...) custom-call(bf16[6,2304]{1,0:T(8,128)(2,1)} %w_qkv.1, ...), custom_call_target="tpu_custom_call" | custom-call | tf_op jit(solution)/shard_map/layer/pallas_call | solution.py:977
  168.1 7.7 %finish.1 = (bf16[4232,512]{1,0:T(8,128)(2,1)}, f32[512,768]{1,0:T(8,128)}, f32[6,2304]{1,0:T(8,128)}, f32[6,768]{1,0:T(8,128)}, f32[6,3072]{1,0:T(8,128)}, /*in...) custom-call(s32[2,16]{1,0:T(2,128)} %pad_add_fusion.route, ...), custom_call_target="tpu_custom_call" | custom-call | tf_op jit(solution)/shard_map/finish/pallas_call | solution.py:1068
  (2 shorter events, 0.0 us)

commit v5 on v3

--- a/solution.py
+++ b/solution.py
@@ -1011,14 +1011,14 @@
         dec[pl.ds(pl.multiple_of(i * 64, 64), 64), :] = blank
         return 0
 
-    lax.fori_loop(0, OUT_ROWS // 64, fill, 0)
+    lax.fori_loop(0, OUT_ROWS // 64, fill, 0, unroll=6)
     dec[OUT_ROWS - 8 :, :] = blank[0:8]
     for k in range(STRIPS):
         perm = perms[k]
         base = STRIP_POS * k - (STRIP_POS * k) % 16
-        filled = dot(perm, jnp.ones((SEG, 128), BF))[:, 0:1]
         loads[k].wait()
-        placed = dot(perm, strips[k])
+        both = dot(perm, jnp.concatenate([strips[k], jnp.ones((SEG, 128), BF)], 1))
+        placed, filled = both[:, 0:DE], both[:, DE : DE + 1]
         dec[base : base + WINDOW] = jnp.where(filled > 0.5, placed, token).astype(BF)
     dec_store = pltpu.make_async_copy(dec, dec_out, sems.at[1])
     dec_store.start()

time: 176 us -> 176 us (level)
  no operation moved by 1% of the time
where the time goes in v5:
time: 176 us
  Pallas kernels  172 us (98%)
  other arithmetic  2.68 us (2%)
    pallas_call x1, Pallas kernels, mega(): pl.pallas_call(kernel, out_shape=(jax.ShapeDtypeStruct((ROWS, D), F32), j...  163 us
    pallas_call x1, Pallas kernels, finish(): pl.pallas_call(finish_kernel, out_shape=(shape((OUT_ROWS, DE), BF), shape...  8.31 us

profile of v5, /device:TPU:0, one launch (start us, length us, event | category | flops | bytes accessed | tf_op | source)
XLA Modules:
  0.0 176.0 jit_solution(7492234928636880889)
XLA Ops:
  0.7 1.4 add_bitcast_fusion.vectors
  2.1 0.7 slice_bitcast_fusion
  2.7 0.1 select_reduce_fusion
  2.8 1.2 pad_add_fusion.route
  4.0 163.5 %layer.1 = (f32[512,768]{1,0:T(8,128)}, bf16[32,2048]{1,0:T(8,128)(2,1)}, bf16[8,272,128]{2,1,0:T(8,128)(2,1)}, f32[1,768]{1,0:T(1,128)}, bf16[16,128,512]{2,1,0...) custom-call(bf16[6,2304]{1,0:T(8,128)(2,1)} %w_qkv.1, ...), custom_call_target="tpu_custom_call" | custom-call | tf_op jit(solution)/shard_map/layer/pallas_call | solution.py:971
  167.5 8.3 %finish.1 = (bf16[4232,512]{1,0:T(8,128)(2,1)}, f32[512,768]{1,0:T(8,128)}, f32[6,2304]{1,0:T(8,128)}, f32[6,768]{1,0:T(8,128)}, f32[6,3072]{1,0:T(8,128)}, /*in...) custom-call(s32[2,16]{1,0:T(2,128)} %pad_add_fusion.route, ...), custom_call_target="tpu_custom_call" | custom-call | tf_op jit(solution)/shard_map/finish/pallas_call | solution.py:1062
  (2 shorter events, 0.0 us)
